TPU v7x, 512 devices: a whole 4x4x16 slice. The times are simulated.
512 devices in a mesh: dp: 16 (over y, x_hi, core), blk: 32 (over x_lo, z).
Axes of the slice: x: 4 (x_hi: 2, x_lo: 2; x = x_hi * 2 + x_lo), y: 4, z: 16, core: 2. Of those that a mesh axis runs over, the one named last changes fastest.
Arguments:
- pre_gelu: bfloat16 [98304, 4096], P(('dp', 'blk')), may hold values from -8 to 8
- out_grad: bfloat16 [98304, 1024], P(('dp', 'blk')), may hold values from -6 to 6
- down_weight: bfloat16 [4096, 1024], P('blk'), may hold values from -0.09375 to 0.09375
Outputs:
- block_out: bfloat16 [98304, 1024], P(('dp', 'blk'))
- pre_grad: bfloat16 [98304, 4096], P(('dp', 'blk'))
- weight_grad: float32 [4096, 1024], P('blk')
All inputs are finite; a program needn't handle non-finite values.
Results may differ from a plain program's by a relative error of at most 0.017.
Values may be sent and summed in bfloat16 or wider, within the bound.
A program may use at most 64 MiB of HBM per device.

v0:
```python
import math
import jax
import jax.numpy as jnp
from jax import lax
from jax.sharding import PartitionSpec as P

SQRT_TWO_PI = 0.7978845608028654
CUBIC = 0.044715


def passed_along(array, axis, by):
    peers = lax.axis_size(axis)
    return lax.ppermute(array, axis, [(i, (i + by) % peers) for i in range(peers)])


def gelu_parts(inputs):
    argument = SQRT_TWO_PI * (inputs + CUBIC * inputs * inputs * inputs)
    tangent = jnp.tanh(argument)
    activation = 0.5 * inputs * (1.0 + tangent)
    derivative = 0.5 * (1.0 + tangent) + 0.5 * inputs * (1.0 - tangent * tangent) * SQRT_TWO_PI * (
        1.0 + 3.0 * CUBIC * inputs * inputs
    )
    return (activation, derivative)


def finish_partial(arrived, own_term):
    rounded = (arrived.astype(jnp.float32) + own_term).astype(jnp.bfloat16)
    return lax.optimization_barrier(rounded).astype(jnp.float32)


def body(pre_gelu, out_grad, down_weight):
    row_count = pre_gelu.shape[0]
    model_width = out_grad.shape[1]
    block_rows = down_weight.shape[0]
    cycle_size = lax.axis_size("blk")
    home_index = lax.axis_index("blk")
    activation, derivative = gelu_parts(pre_gelu.astype(jnp.float32))
    hidden = activation.astype(jnp.bfloat16)

    def visit(weight, column, carried):
        out_total, grad_buffer = carried
        part_width = weight.shape[0]
        hidden_part = lax.dynamic_slice_in_dim(hidden, column, part_width, 1)
        slope_part = lax.dynamic_slice_in_dim(derivative, column, part_width, 1)
        out_total = out_total + jnp.dot(hidden_part, weight, preferred_element_type=jnp.float32)
        d_hidden = lax.dot_general(
            out_grad, weight, (((1,), (1,)), ((), ())), preferred_element_type=jnp.float32
        )
        grad_buffer = lax.dynamic_update_slice_in_dim(
            grad_buffer, (d_hidden * slope_part).astype(jnp.bfloat16), column, 1
        )
        contribution = lax.dot_general(
            hidden_part, out_grad, (((0,), (0,)), ((), ())), preferred_element_type=jnp.float32
        )
        return ((out_total, grad_buffer), contribution)

    carried = (
        jnp.zeros((row_count, model_width), jnp.float32),
        jnp.zeros(pre_gelu.shape, jnp.bfloat16),
    )

    def pass_weight(weight):
        return passed_along(weight, "blk", 1)

    def pass_grad(partial_value):
        return passed_along(partial_value, "blk", 1)

    carried, own_term = visit(down_weight, home_index * block_rows, carried)
    weight = pass_weight(down_weight)
    carried, contribution = visit(weight, jnp.mod(home_index - 1, cycle_size) * block_rows, carried)
    partial_value = contribution.astype(jnp.bfloat16)

    def one_stop(stop_number, loop_state):
        weight, partial_value, carried = loop_state
        weight = pass_weight(weight)
        carried, contribution = visit(
            weight, jnp.mod(home_index - stop_number, cycle_size) * block_rows, carried
        )
        partial_value = (pass_grad(partial_value).astype(jnp.float32) + contribution).astype(
            jnp.bfloat16
        )
        return (weight, partial_value, carried)

    weight, partial_value, carried = lax.fori_loop(
        2, cycle_size, one_stop, (weight, partial_value, carried)
    )
    finished = finish_partial(pass_grad(partial_value), own_term)
    out_total, grad_buffer = carried
    summed = lax.psum(finished.astype(jnp.bfloat16), "dp").astype(jnp.float32)
    token_count = row_count * cycle_size * lax.axis_size("dp")
    return (out_total.astype(jnp.bfloat16), grad_buffer, summed / math.sqrt(token_count))


def solution(mesh):
    in_specs = (P(("dp", "blk"), None), P(("dp", "blk"), None), P("blk", None))
    out_specs = (P(("dp", "blk"), None), P(("dp", "blk"), None), P("blk", None))
    return jax.shard_map(body, mesh=mesh, in_specs=in_specs, out_specs=out_specs, check_vma=False)
```

profile of v0, /device:TPU:1, one launch (start us, length us, event | category | flops | bytes accessed | tf_op | source)
XLA Modules:
  0.0 725.1 jit_solution(6232754334397640442)
XLA Ops:
  7.2 4.4 collective-permute-start.2
  11.6 4.5 fusion.14
  20.4 5.9 collective-permute-done.2
  28.4 498.7 %while.21 = (s32[]{:T(128)}, bf16[128,1024]{1,0:T(8,128)(2,1)S(1)}, bf16[128,1024]{1,0:T(8,128)(2,1)}, f32[192,1024]{1,0:T(8,128)S(1)}, bf16[192,4096]{1,0:T(8,1...) while((s32[]{:T(128)}, bf16[128,1024]{1,0:T(8,128)(2,1)S(1)}, ...), condition=%wide.region_1.2_spmd, body=%wide.region_0.1_spmd.sunk | while | flops 151633936 | bytes 6275492 | solution.py:84
  32.3 6.7 collective-permute-done
  39.3 5.3 collective-permute-done.1
  51.2 5.8 collective-permute-done
  57.3 5.3 collective-permute-done.1
  69.2 5.3 collective-permute-done
  74.9 4.8 collective-permute-done.1
  86.3 5.3 collective-permute-done
  91.9 3.9 collective-permute-done.1
  102.4 5.3 collective-permute-done
  108.1 3.0 collective-permute-done.1
  117.7 5.3 collective-permute-done
  123.3 2.5 collective-permute-done.1
  132.5 5.3 collective-permute-done
  138.1 2.5 collective-permute-done.1
  145.3 3.0 collective-permute-start.1
  148.3 4.2 collective-permute-done
  158.1 2.7 collective-permute-start
  160.9 4.0 collective-permute-start.1
  167.6 2.7 collective-permute-done.1
  173.1 3.9 collective-permute-start
  177.0 4.4 collective-permute-start.1
  183.0 3.4 collective-permute-done.1
  189.1 5.1 collective-permute-start
  194.2 4.0 collective-permute-start.1
  199.3 4.4 collective-permute-done.1
  206.4 4.5 collective-permute-start
  211.0 4.0 collective-permute-start.1
  215.9 4.5 collective-permute-done.1
  223.2 2.9 collective-permute-start
  226.1 4.0 collective-permute-start.1
  232.7 2.8 collective-permute-done.1
  240.2 4.0 collective-permute-start.1
  244.2 4.8 collective-permute-done
  258.5 8.2 %collective-permute-done = bf16[128,1024]{1,0:T(8,128)(2,1)S(1)} collective-permute-done((bf16[128,1024]{1,0:T(8,128)(2,1)S(1)}, bf16[128,1024]{1,0:T(8,128)(2,1)S(1)}, u32[]{:S(2)}, u32[]{:S(2)}) %collective-permute-start) | collective-permute-done | bytes 262176 | tf_op jit(solution)/shard_map/while/body/eval_jaxpr/ppermute | solution.py:13
  267.0 5.3 collective-permute-done.1
  278.9 7.3 %collective-permute-done = bf16[128,1024]{1,0:T(8,128)(2,1)S(1)} collective-permute-done((bf16[128,1024]{1,0:T(8,128)(2,1)S(1)}, bf16[128,1024]{1,0:T(8,128)(2,1)S(1)}, u32[]{:S(2)}, u32[]{:S(2)}) %collective-permute-start) | collective-permute-done | bytes 262176 | tf_op jit(solution)/shard_map/while/body/eval_jaxpr/ppermute | solution.py:13
  286.5 5.3 collective-permute-done.1
  298.5 6.4 collective-permute-done
  305.2 5.3 collective-permute-done.1
  317.1 5.3 collective-permute-done
  322.7 5.5 collective-permute-done.1
  334.8 5.3 collective-permute-done
  340.5 4.5 collective-permute-done.1
  351.6 5.3 collective-permute-done
  357.3 3.6 collective-permute-done.1
  367.5 5.3 collective-permute-done
  373.1 2.5 collective-permute-done.1
  382.3 5.5 collective-permute-done
  397.2 5.3 collective-permute-done
  412.0 5.3 collective-permute-done
  426.7 5.3 collective-permute-done
  441.5 6.3 collective-permute-done
  457.5 7.1 collective-permute-done
  474.0 8.5 %collective-permute-done = bf16[128,1024]{1,0:T(8,128)(2,1)S(1)} collective-permute-done((bf16[128,1024]{1,0:T(8,128)(2,1)S(1)}, bf16[128,1024]{1,0:T(8,128)(2,1)S(1)}, u32[]{:S(2)}, u32[]{:S(2)}) %collective-permute-start) | collective-permute-done | bytes 262176 | tf_op jit(solution)/shard_map/while/body/eval_jaxpr/ppermute | solution.py:13
  491.9 8.5 %collective-permute-done = bf16[128,1024]{1,0:T(8,128)(2,1)S(1)} collective-permute-done((bf16[128,1024]{1,0:T(8,128)(2,1)S(1)}, bf16[128,1024]{1,0:T(8,128)(2,1)S(1)}, u32[]{:S(2)}, u32[]{:S(2)}) %collective-permute-start) | collective-permute-done | bytes 262176 | tf_op jit(solution)/shard_map/while/body/eval_jaxpr/ppermute | solution.py:13
  500.7 3.5 collective-permute-done.1
  510.9 8.3 %collective-permute-done = bf16[128,1024]{1,0:T(8,128)(2,1)S(1)} collective-permute-done((bf16[128,1024]{1,0:T(8,128)(2,1)S(1)}, bf16[128,1024]{1,0:T(8,128)(2,1)S(1)}, u32[]{:S(2)}, u32[]{:S(2)}) %collective-permute-start) | collective-permute-done | bytes 262176 | tf_op jit(solution)/shard_map/while/body/eval_jaxpr/ppermute | solution.py:13
  519.5 4.8 collective-permute-done.1
  529.2 9.8 %collective-permute-done.3 = bf16[128,1024]{1,0:T(8,128)(2,1)S(1)} collective-permute-done((bf16[128,1024]{1,0:T(8,128)(2,1)}, bf16[128,1024]{1,0:T(8,128)(2,1)S(1)}, u32[]{:S(2)}, u32[]{:S(2)}) %collective-permute-start.3) | collective-permute-done | bytes 262176 | tf_op jit(solution)/shard_map/ppermute | solution.py:13
  540.6 175.8 %all-reduce.2.cloned.1.call-done = bf16[128,1024]{1,0:T(8,128)(2,1)} async-done(((bf16[128,1024]{1,0:T(8,128)(2,1)}), bf16[128,1024]{1,0:T(8,128)(2,1)}) %all-reduce.2.cloned.1.call-update) | async-done | bytes 262160 | tf_op jit(solution)/shard_map/psum | solution.py:89
  (199 shorter events, 225.2 us)
Async XLA Ops:
  7.2 709.2 %all-reduce.2.cloned.1.call-start = ((), (), s32[]{:S(2)}) async-start(), calls=%async_computation | async-start | bytes 524288 | tf_op jit(solution)/shard_map/psum | solution.py:89
  7.2 19.1 %collective-permute-start.2 = (bf16[128,1024]{1,0:T(8,128)(2,1)}, bf16[128,1024]{1,0:T(8,128)(2,1)S(1)}, u32[]{:S(2)}, u32[]{:S(2)}) collective-permute-start(bf16[128,1024]{1,0:T(8,128)(2,1)} %param.7), channel_id=1, source_target_pairs={{0,1},{1,2},{2,3},{3,4},{4,5},{5,6},{6,7},{7,8},{8,9},{9,10},{10,1... | collective-permute-start | bytes 786440 | tf_op jit(solution)/shard_map/ppermute | solution.py:13
  11.6 5.8 copy-start
  28.4 10.6 %collective-permute-start = (bf16[128,1024]{1,0:T(8,128)(2,1)S(1)}, bf16[128,1024]{1,0:T(8,128)(2,1)S(1)}, u32[]{:S(2)}, u32[]{:S(2)}) collective-permute-start(bf16[128,1024]{1,0:T(8,128)(2,1)S(1)} %get-tuple-element.321), channel_id=1, source_target_pairs={{0,1},{1,2},{2,3},{3,4},{4,5},{5,6},{6,7},{7,8},{8,9},{9,10},{10,1... | collective-permute-start | bytes 786440 | tf_op jit(solution)/shard_map/while/body/eval_jaxpr/ppermute | solution.py:13
  30.3 14.3 %collective-permute-start.1 = (bf16[128,1024]{1,0:T(8,128)(2,1)}, bf16[128,1024]{1,0:T(8,128)(2,1)S(1)}, u32[]{:S(2)}, u32[]{:S(2)}) collective-permute-start(bf16[128,1024]{1,0:T(8,128)(2,1)} %get-tuple-element.322), channel_id=1, source_target_pairs={{0,1},{1,2},{2,3},{3,4},{4,5},{5,6},{6,7},{7,8},{8,9},{9,10},{10,1... | collective-permute-start | bytes 786440 | tf_op jit(solution)/shard_map/while/body/eval_jaxpr/ppermute | solution.py:13
  47.3 9.6 %collective-permute-start = (bf16[128,1024]{1,0:T(8,128)(2,1)S(1)}, bf16[128,1024]{1,0:T(8,128)(2,1)S(1)}, u32[]{:S(2)}, u32[]{:S(2)}) collective-permute-start(bf16[128,1024]{1,0:T(8,128)(2,1)S(1)} %get-tuple-element.321), channel_id=1, source_target_pairs={{0,1},{1,2},{2,3},{3,4},{4,5},{5,6},{6,7},{7,8},{8,9},{9,10},{10,1... | collective-permute-start | bytes 786440 | tf_op jit(solution)/shard_map/while/body/eval_jaxpr/ppermute | solution.py:13
  49.3 13.3 %collective-permute-start.1 = (bf16[128,1024]{1,0:T(8,128)(2,1)}, bf16[128,1024]{1,0:T(8,128)(2,1)S(1)}, u32[]{:S(2)}, u32[]{:S(2)}) collective-permute-start(bf16[128,1024]{1,0:T(8,128)(2,1)} %get-tuple-element.322), channel_id=1, source_target_pairs={{0,1},{1,2},{2,3},{3,4},{4,5},{5,6},{6,7},{7,8},{8,9},{9,10},{10,1... | collective-permute-start | bytes 786440 | tf_op jit(solution)/shard_map/while/body/eval_jaxpr/ppermute | solution.py:13
  65.3 9.2 %collective-permute-start = (bf16[128,1024]{1,0:T(8,128)(2,1)S(1)}, bf16[128,1024]{1,0:T(8,128)(2,1)S(1)}, u32[]{:S(2)}, u32[]{:S(2)}) collective-permute-start(bf16[128,1024]{1,0:T(8,128)(2,1)S(1)} %get-tuple-element.321), channel_id=1, source_target_pairs={{0,1},{1,2},{2,3},{3,4},{4,5},{5,6},{6,7},{7,8},{8,9},{9,10},{10,1... | collective-permute-start | bytes 786440 | tf_op jit(solution)/shard_map/while/body/eval_jaxpr/ppermute | solution.py:13
  67.3 12.4 %collective-permute-start.1 = (bf16[128,1024]{1,0:T(8,128)(2,1)}, bf16[128,1024]{1,0:T(8,128)(2,1)S(1)}, u32[]{:S(2)}, u32[]{:S(2)}) collective-permute-start(bf16[128,1024]{1,0:T(8,128)(2,1)} %get-tuple-element.322), channel_id=1, source_target_pairs={{0,1},{1,2},{2,3},{3,4},{4,5},{5,6},{6,7},{7,8},{8,9},{9,10},{10,1... | collective-permute-start | bytes 786440 | tf_op jit(solution)/shard_map/while/body/eval_jaxpr/ppermute | solution.py:13
  82.4 9.2 %collective-permute-start = (bf16[128,1024]{1,0:T(8,128)(2,1)S(1)}, bf16[128,1024]{1,0:T(8,128)(2,1)S(1)}, u32[]{:S(2)}, u32[]{:S(2)}) collective-permute-start(bf16[128,1024]{1,0:T(8,128)(2,1)S(1)} %get-tuple-element.321), channel_id=1, source_target_pairs={{0,1},{1,2},{2,3},{3,4},{4,5},{5,6},{6,7},{7,8},{8,9},{9,10},{10,1... | collective-permute-start | bytes 786440 | tf_op jit(solution)/shard_map/while/body/eval_jaxpr/ppermute | solution.py:13
  84.3 11.5 %collective-permute-start.1 = (bf16[128,1024]{1,0:T(8,128)(2,1)}, bf16[128,1024]{1,0:T(8,128)(2,1)S(1)}, u32[]{:S(2)}, u32[]{:S(2)}) collective-permute-start(bf16[128,1024]{1,0:T(8,128)(2,1)} %get-tuple-element.322), channel_id=1, source_target_pairs={{0,1},{1,2},{2,3},{3,4},{4,5},{5,6},{6,7},{7,8},{8,9},{9,10},{10,1... | collective-permute-start | bytes 786440 | tf_op jit(solution)/shard_map/while/body/eval_jaxpr/ppermute | solution.py:13
  98.6 9.2 %collective-permute-start = (bf16[128,1024]{1,0:T(8,128)(2,1)S(1)}, bf16[128,1024]{1,0:T(8,128)(2,1)S(1)}, u32[]{:S(2)}, u32[]{:S(2)}) collective-permute-start(bf16[128,1024]{1,0:T(8,128)(2,1)S(1)} %get-tuple-element.321), channel_id=1, source_target_pairs={{0,1},{1,2},{2,3},{3,4},{4,5},{5,6},{6,7},{7,8},{8,9},{9,10},{10,1... | collective-permute-start | bytes 786440 | tf_op jit(solution)/shard_map/while/body/eval_jaxpr/ppermute | solution.py:13
  100.5 10.6 %collective-permute-start.1 = (bf16[128,1024]{1,0:T(8,128)(2,1)}, bf16[128,1024]{1,0:T(8,128)(2,1)S(1)}, u32[]{:S(2)}, u32[]{:S(2)}) collective-permute-start(bf16[128,1024]{1,0:T(8,128)(2,1)} %get-tuple-element.322), channel_id=1, source_target_pairs={{0,1},{1,2},{2,3},{3,4},{4,5},{5,6},{6,7},{7,8},{8,9},{9,10},{10,1... | collective-permute-start | bytes 786440 | tf_op jit(solution)/shard_map/while/body/eval_jaxpr/ppermute | solution.py:13
  113.8 9.2 %collective-permute-start = (bf16[128,1024]{1,0:T(8,128)(2,1)S(1)}, bf16[128,1024]{1,0:T(8,128)(2,1)S(1)}, u32[]{:S(2)}, u32[]{:S(2)}) collective-permute-start(bf16[128,1024]{1,0:T(8,128)(2,1)S(1)} %get-tuple-element.321), channel_id=1, source_target_pairs={{0,1},{1,2},{2,3},{3,4},{4,5},{5,6},{6,7},{7,8},{8,9},{9,10},{10,1... | collective-permute-start | bytes 786440 | tf_op jit(solution)/shard_map/while/body/eval_jaxpr/ppermute | solution.py:13
  115.7 10.1 %collective-permute-start.1 = (bf16[128,1024]{1,0:T(8,128)(2,1)}, bf16[128,1024]{1,0:T(8,128)(2,1)S(1)}, u32[]{:S(2)}, u32[]{:S(2)}) collective-permute-start(bf16[128,1024]{1,0:T(8,128)(2,1)} %get-tuple-element.322), channel_id=1, source_target_pairs={{0,1},{1,2},{2,3},{3,4},{4,5},{5,6},{6,7},{7,8},{8,9},{9,10},{10,1... | collective-permute-start | bytes 786440 | tf_op jit(solution)/shard_map/while/body/eval_jaxpr/ppermute | solution.py:13
  128.6 9.2 %collective-permute-start = (bf16[128,1024]{1,0:T(8,128)(2,1)S(1)}, bf16[128,1024]{1,0:T(8,128)(2,1)S(1)}, u32[]{:S(2)}, u32[]{:S(2)}) collective-permute-start(bf16[128,1024]{1,0:T(8,128)(2,1)S(1)} %get-tuple-element.321), channel_id=1, source_target_pairs={{0,1},{1,2},{2,3},{3,4},{4,5},{5,6},{6,7},{7,8},{8,9},{9,10},{10,1... | collective-permute-start | bytes 786440 | tf_op jit(solution)/shard_map/while/body/eval_jaxpr/ppermute | solution.py:13
  130.5 10.1 %collective-permute-start.1 = (bf16[128,1024]{1,0:T(8,128)(2,1)}, bf16[128,1024]{1,0:T(8,128)(2,1)S(1)}, u32[]{:S(2)}, u32[]{:S(2)}) collective-permute-start(bf16[128,1024]{1,0:T(8,128)(2,1)} %get-tuple-element.322), channel_id=1, source_target_pairs={{0,1},{1,2},{2,3},{3,4},{4,5},{5,6},{6,7},{7,8},{8,9},{9,10},{10,1... | collective-permute-start | bytes 786440 | tf_op jit(solution)/shard_map/while/body/eval_jaxpr/ppermute | solution.py:13
  143.4 9.2 %collective-permute-start = (bf16[128,1024]{1,0:T(8,128)(2,1)S(1)}, bf16[128,1024]{1,0:T(8,128)(2,1)S(1)}, u32[]{:S(2)}, u32[]{:S(2)}) collective-permute-start(bf16[128,1024]{1,0:T(8,128)(2,1)S(1)} %get-tuple-element.321), channel_id=1, source_target_pairs={{0,1},{1,2},{2,3},{3,4},{4,5},{5,6},{6,7},{7,8},{8,9},{9,10},{10,1... | collective-permute-start | bytes 786440 | tf_op jit(solution)/shard_map/while/body/eval_jaxpr/ppermute | solution.py:13
  145.3 10.1 %collective-permute-start.1 = (bf16[128,1024]{1,0:T(8,128)(2,1)}, bf16[128,1024]{1,0:T(8,128)(2,1)S(1)}, u32[]{:S(2)}, u32[]{:S(2)}) collective-permute-start(bf16[128,1024]{1,0:T(8,128)(2,1)} %get-tuple-element.322), channel_id=1, source_target_pairs={{0,1},{1,2},{2,3},{3,4},{4,5},{5,6},{6,7},{7,8},{8,9},{9,10},{10,1... | collective-permute-start | bytes 786440 | tf_op jit(solution)/shard_map/while/body/eval_jaxpr/ppermute | solution.py:13
  158.1 9.2 %collective-permute-start = (bf16[128,1024]{1,0:T(8,128)(2,1)S(1)}, bf16[128,1024]{1,0:T(8,128)(2,1)S(1)}, u32[]{:S(2)}, u32[]{:S(2)}) collective-permute-start(bf16[128,1024]{1,0:T(8,128)(2,1)S(1)} %get-tuple-element.321), channel_id=1, source_target_pairs={{0,1},{1,2},{2,3},{3,4},{4,5},{5,6},{6,7},{7,8},{8,9},{9,10},{10,1... | collective-permute-start | bytes 786440 | tf_op jit(solution)/shard_map/while/body/eval_jaxpr/ppermute | solution.py:13
  160.9 9.4 %collective-permute-start.1 = (bf16[128,1024]{1,0:T(8,128)(2,1)}, bf16[128,1024]{1,0:T(8,128)(2,1)S(1)}, u32[]{:S(2)}, u32[]{:S(2)}) collective-permute-start(bf16[128,1024]{1,0:T(8,128)(2,1)} %get-tuple-element.322), channel_id=1, source_target_pairs={{0,1},{1,2},{2,3},{3,4},{4,5},{5,6},{6,7},{7,8},{8,9},{9,10},{10,1... | collective-permute-start | bytes 786440 | tf_op jit(solution)/shard_map/while/body/eval_jaxpr/ppermute | solution.py:13
  173.1 9.6 %collective-permute-start = (bf16[128,1024]{1,0:T(8,128)(2,1)S(1)}, bf16[128,1024]{1,0:T(8,128)(2,1)S(1)}, u32[]{:S(2)}, u32[]{:S(2)}) collective-permute-start(bf16[128,1024]{1,0:T(8,128)(2,1)S(1)} %get-tuple-element.321), channel_id=1, source_target_pairs={{0,1},{1,2},{2,3},{3,4},{4,5},{5,6},{6,7},{7,8},{8,9},{9,10},{10,1... | collective-permute-start | bytes 786440 | tf_op jit(solution)/shard_map/while/body/eval_jaxpr/ppermute | solution.py:13
  177.0 9.4 %collective-permute-start.1 = (bf16[128,1024]{1,0:T(8,128)(2,1)}, bf16[128,1024]{1,0:T(8,128)(2,1)S(1)}, u32[]{:S(2)}, u32[]{:S(2)}) collective-permute-start(bf16[128,1024]{1,0:T(8,128)(2,1)} %get-tuple-element.322), channel_id=1, source_target_pairs={{0,1},{1,2},{2,3},{3,4},{4,5},{5,6},{6,7},{7,8},{8,9},{9,10},{10,1... | collective-permute-start | bytes 786440 | tf_op jit(solution)/shard_map/while/body/eval_jaxpr/ppermute | solution.py:13
  189.1 9.9 %collective-permute-start = (bf16[128,1024]{1,0:T(8,128)(2,1)S(1)}, bf16[128,1024]{1,0:T(8,128)(2,1)S(1)}, u32[]{:S(2)}, u32[]{:S(2)}) collective-permute-start(bf16[128,1024]{1,0:T(8,128)(2,1)S(1)} %get-tuple-element.321), channel_id=1, source_target_pairs={{0,1},{1,2},{2,3},{3,4},{4,5},{5,6},{6,7},{7,8},{8,9},{9,10},{10,1... | collective-permute-start | bytes 786440 | tf_op jit(solution)/shard_map/while/body/eval_jaxpr/ppermute | solution.py:13
  194.2 9.4 %collective-permute-start.1 = (bf16[128,1024]{1,0:T(8,128)(2,1)}, bf16[128,1024]{1,0:T(8,128)(2,1)S(1)}, u32[]{:S(2)}, u32[]{:S(2)}) collective-permute-start(bf16[128,1024]{1,0:T(8,128)(2,1)} %get-tuple-element.322), channel_id=1, source_target_pairs={{0,1},{1,2},{2,3},{3,4},{4,5},{5,6},{6,7},{7,8},{8,9},{9,10},{10,1... | collective-permute-start | bytes 786440 | tf_op jit(solution)/shard_map/while/body/eval_jaxpr/ppermute | solution.py:13
  206.4 9.2 %collective-permute-start = (bf16[128,1024]{1,0:T(8,128)(2,1)S(1)}, bf16[128,1024]{1,0:T(8,128)(2,1)S(1)}, u32[]{:S(2)}, u32[]{:S(2)}) collective-permute-start(bf16[128,1024]{1,0:T(8,128)(2,1)S(1)} %get-tuple-element.321), channel_id=1, source_target_pairs={{0,1},{1,2},{2,3},{3,4},{4,5},{5,6},{6,7},{7,8},{8,9},{9,10},{10,1... | collective-permute-start | bytes 786440 | tf_op jit(solution)/shard_map/while/body/eval_jaxpr/ppermute | solution.py:13
  211.0 9.4 %collective-permute-start.1 = (bf16[128,1024]{1,0:T(8,128)(2,1)}, bf16[128,1024]{1,0:T(8,128)(2,1)S(1)}, u32[]{:S(2)}, u32[]{:S(2)}) collective-permute-start(bf16[128,1024]{1,0:T(8,128)(2,1)} %get-tuple-element.322), channel_id=1, source_target_pairs={{0,1},{1,2},{2,3},{3,4},{4,5},{5,6},{6,7},{7,8},{8,9},{9,10},{10,1... | collective-permute-start | bytes 786440 | tf_op jit(solution)/shard_map/while/body/eval_jaxpr/ppermute | solution.py:13
  223.2 9.2 %collective-permute-start = (bf16[128,1024]{1,0:T(8,128)(2,1)S(1)}, bf16[128,1024]{1,0:T(8,128)(2,1)S(1)}, u32[]{:S(2)}, u32[]{:S(2)}) collective-permute-start(bf16[128,1024]{1,0:T(8,128)(2,1)S(1)} %get-tuple-element.321), channel_id=1, source_target_pairs={{0,1},{1,2},{2,3},{3,4},{4,5},{5,6},{6,7},{7,8},{8,9},{9,10},{10,1... | collective-permute-start | bytes 786440 | tf_op jit(solution)/shard_map/while/body/eval_jaxpr/ppermute | solution.py:13
  226.1 9.4 %collective-permute-start.1 = (bf16[128,1024]{1,0:T(8,128)(2,1)}, bf16[128,1024]{1,0:T(8,128)(2,1)S(1)}, u32[]{:S(2)}, u32[]{:S(2)}) collective-permute-start(bf16[128,1024]{1,0:T(8,128)(2,1)} %get-tuple-element.322), channel_id=1, source_target_pairs={{0,1},{1,2},{2,3},{3,4},{4,5},{5,6},{6,7},{7,8},{8,9},{9,10},{10,1... | collective-permute-start | bytes 786440 | tf_op jit(solution)/shard_map/while/body/eval_jaxpr/ppermute | solution.py:13
  238.2 10.8 %collective-permute-start = (bf16[128,1024]{1,0:T(8,128)(2,1)S(1)}, bf16[128,1024]{1,0:T(8,128)(2,1)S(1)}, u32[]{:S(2)}, u32[]{:S(2)}) collective-permute-start(bf16[128,1024]{1,0:T(8,128)(2,1)S(1)} %get-tuple-element.321), channel_id=1, source_target_pairs={{0,1},{1,2},{2,3},{3,4},{4,5},{5,6},{6,7},{7,8},{8,9},{9,10},{10,1... | collective-permute-start | bytes 786440 | tf_op jit(solution)/shard_map/while/body/eval_jaxpr/ppermute | solution.py:13
  240.2 11.6 %collective-permute-start.1 = (bf16[128,1024]{1,0:T(8,128)(2,1)}, bf16[128,1024]{1,0:T(8,128)(2,1)S(1)}, u32[]{:S(2)}, u32[]{:S(2)}) collective-permute-start(bf16[128,1024]{1,0:T(8,128)(2,1)} %get-tuple-element.322), channel_id=1, source_target_pairs={{0,1},{1,2},{2,3},{3,4},{4,5},{5,6},{6,7},{7,8},{8,9},{9,10},{10,1... | collective-permute-start | bytes 786440 | tf_op jit(solution)/shard_map/while/body/eval_jaxpr/ppermute | solution.py:13
  254.6 12.1 %collective-permute-start = (bf16[128,1024]{1,0:T(8,128)(2,1)S(1)}, bf16[128,1024]{1,0:T(8,128)(2,1)S(1)}, u32[]{:S(2)}, u32[]{:S(2)}) collective-permute-start(bf16[128,1024]{1,0:T(8,128)(2,1)S(1)} %get-tuple-element.321), channel_id=1, source_target_pairs={{0,1},{1,2},{2,3},{3,4},{4,5},{5,6},{6,7},{7,8},{8,9},{9,10},{10,1... | collective-permute-start | bytes 786440 | tf_op jit(solution)/shard_map/while/body/eval_jaxpr/ppermute | solution.py:13
  256.5 15.8 %collective-permute-start.1 = (bf16[128,1024]{1,0:T(8,128)(2,1)}, bf16[128,1024]{1,0:T(8,128)(2,1)S(1)}, u32[]{:S(2)}, u32[]{:S(2)}) collective-permute-start(bf16[128,1024]{1,0:T(8,128)(2,1)} %get-tuple-element.322), channel_id=1, source_target_pairs={{0,1},{1,2},{2,3},{3,4},{4,5},{5,6},{6,7},{7,8},{8,9},{9,10},{10,1... | collective-permute-start | bytes 786440 | tf_op jit(solution)/shard_map/while/body/eval_jaxpr/ppermute | solution.py:13
  275.0 11.2 %collective-permute-start = (bf16[128,1024]{1,0:T(8,128)(2,1)S(1)}, bf16[128,1024]{1,0:T(8,128)(2,1)S(1)}, u32[]{:S(2)}, u32[]{:S(2)}) collective-permute-start(bf16[128,1024]{1,0:T(8,128)(2,1)S(1)} %get-tuple-element.321), channel_id=1, source_target_pairs={{0,1},{1,2},{2,3},{3,4},{4,5},{5,6},{6,7},{7,8},{8,9},{9,10},{10,1... | collective-permute-start | bytes 786440 | tf_op jit(solution)/shard_map/while/body/eval_jaxpr/ppermute | solution.py:13
  276.9 14.9 %collective-permute-start.1 = (bf16[128,1024]{1,0:T(8,128)(2,1)}, bf16[128,1024]{1,0:T(8,128)(2,1)S(1)}, u32[]{:S(2)}, u32[]{:S(2)}) collective-permute-start(bf16[128,1024]{1,0:T(8,128)(2,1)} %get-tuple-element.322), channel_id=1, source_target_pairs={{0,1},{1,2},{2,3},{3,4},{4,5},{5,6},{6,7},{7,8},{8,9},{9,10},{10,1... | collective-permute-start | bytes 786440 | tf_op jit(solution)/shard_map/while/body/eval_jaxpr/ppermute | solution.py:13
  294.6 10.3 %collective-permute-start = (bf16[128,1024]{1,0:T(8,128)(2,1)S(1)}, bf16[128,1024]{1,0:T(8,128)(2,1)S(1)}, u32[]{:S(2)}, u32[]{:S(2)}) collective-permute-start(bf16[128,1024]{1,0:T(8,128)(2,1)S(1)} %get-tuple-element.321), channel_id=1, source_target_pairs={{0,1},{1,2},{2,3},{3,4},{4,5},{5,6},{6,7},{7,8},{8,9},{9,10},{10,1... | collective-permute-start | bytes 786440 | tf_op jit(solution)/shard_map/while/body/eval_jaxpr/ppermute | solution.py:13
  296.5 14.0 %collective-permute-start.1 = (bf16[128,1024]{1,0:T(8,128)(2,1)}, bf16[128,1024]{1,0:T(8,128)(2,1)S(1)}, u32[]{:S(2)}, u32[]{:S(2)}) collective-permute-start(bf16[128,1024]{1,0:T(8,128)(2,1)} %get-tuple-element.322), channel_id=1, source_target_pairs={{0,1},{1,2},{2,3},{3,4},{4,5},{5,6},{6,7},{7,8},{8,9},{9,10},{10,1... | collective-permute-start | bytes 786440 | tf_op jit(solution)/shard_map/while/body/eval_jaxpr/ppermute | solution.py:13
  313.2 9.2 %collective-permute-start = (bf16[128,1024]{1,0:T(8,128)(2,1)S(1)}, bf16[128,1024]{1,0:T(8,128)(2,1)S(1)}, u32[]{:S(2)}, u32[]{:S(2)}) collective-permute-start(bf16[128,1024]{1,0:T(8,128)(2,1)S(1)} %get-tuple-element.321), channel_id=1, source_target_pairs={{0,1},{1,2},{2,3},{3,4},{4,5},{5,6},{6,7},{7,8},{8,9},{9,10},{10,1... | collective-permute-start | bytes 786440 | tf_op jit(solution)/shard_map/while/body/eval_jaxpr/ppermute | solution.py:13
  315.1 13.1 %collective-permute-start.1 = (bf16[128,1024]{1,0:T(8,128)(2,1)}, bf16[128,1024]{1,0:T(8,128)(2,1)S(1)}, u32[]{:S(2)}, u32[]{:S(2)}) collective-permute-start(bf16[128,1024]{1,0:T(8,128)(2,1)} %get-tuple-element.322), channel_id=1, source_target_pairs={{0,1},{1,2},{2,3},{3,4},{4,5},{5,6},{6,7},{7,8},{8,9},{9,10},{10,1... | collective-permute-start | bytes 786440 | tf_op jit(solution)/shard_map/while/body/eval_jaxpr/ppermute | solution.py:13
  330.9 9.2 %collective-permute-start = (bf16[128,1024]{1,0:T(8,128)(2,1)S(1)}, bf16[128,1024]{1,0:T(8,128)(2,1)S(1)}, u32[]{:S(2)}, u32[]{:S(2)}) collective-permute-start(bf16[128,1024]{1,0:T(8,128)(2,1)S(1)} %get-tuple-element.321), channel_id=1, source_target_pairs={{0,1},{1,2},{2,3},{3,4},{4,5},{5,6},{6,7},{7,8},{8,9},{9,10},{10,1... | collective-permute-start | bytes 786440 | tf_op jit(solution)/shard_map/while/body/eval_jaxpr/ppermute | solution.py:13
  332.9 12.1 %collective-permute-start.1 = (bf16[128,1024]{1,0:T(8,128)(2,1)}, bf16[128,1024]{1,0:T(8,128)(2,1)S(1)}, u32[]{:S(2)}, u32[]{:S(2)}) collective-permute-start(bf16[128,1024]{1,0:T(8,128)(2,1)} %get-tuple-element.322), channel_id=1, source_target_pairs={{0,1},{1,2},{2,3},{3,4},{4,5},{5,6},{6,7},{7,8},{8,9},{9,10},{10,1... | collective-permute-start | bytes 786440 | tf_op jit(solution)/shard_map/while/body/eval_jaxpr/ppermute | solution.py:13
  347.7 9.2 %collective-permute-start = (bf16[128,1024]{1,0:T(8,128)(2,1)S(1)}, bf16[128,1024]{1,0:T(8,128)(2,1)S(1)}, u32[]{:S(2)}, u32[]{:S(2)}) collective-permute-start(bf16[128,1024]{1,0:T(8,128)(2,1)S(1)} %get-tuple-element.321), channel_id=1, source_target_pairs={{0,1},{1,2},{2,3},{3,4},{4,5},{5,6},{6,7},{7,8},{8,9},{9,10},{10,1... | collective-permute-start | bytes 786440 | tf_op jit(solution)/shard_map/while/body/eval_jaxpr/ppermute | solution.py:13
  349.7 11.2 %collective-permute-start.1 = (bf16[128,1024]{1,0:T(8,128)(2,1)}, bf16[128,1024]{1,0:T(8,128)(2,1)S(1)}, u32[]{:S(2)}, u32[]{:S(2)}) collective-permute-start(bf16[128,1024]{1,0:T(8,128)(2,1)} %get-tuple-element.322), channel_id=1, source_target_pairs={{0,1},{1,2},{2,3},{3,4},{4,5},{5,6},{6,7},{7,8},{8,9},{9,10},{10,1... | collective-permute-start | bytes 786440 | tf_op jit(solution)/shard_map/while/body/eval_jaxpr/ppermute | solution.py:13
  363.6 9.2 %collective-permute-start = (bf16[128,1024]{1,0:T(8,128)(2,1)S(1)}, bf16[128,1024]{1,0:T(8,128)(2,1)S(1)}, u32[]{:S(2)}, u32[]{:S(2)}) collective-permute-start(bf16[128,1024]{1,0:T(8,128)(2,1)S(1)} %get-tuple-element.321), channel_id=1, source_target_pairs={{0,1},{1,2},{2,3},{3,4},{4,5},{5,6},{6,7},{7,8},{8,9},{9,10},{10,1... | collective-permute-start | bytes 786440 | tf_op jit(solution)/shard_map/while/body/eval_jaxpr/ppermute | solution.py:13
  365.5 10.1 %collective-permute-start.1 = (bf16[128,1024]{1,0:T(8,128)(2,1)}, bf16[128,1024]{1,0:T(8,128)(2,1)S(1)}, u32[]{:S(2)}, u32[]{:S(2)}) collective-permute-start(bf16[128,1024]{1,0:T(8,128)(2,1)} %get-tuple-element.322), channel_id=1, source_target_pairs={{0,1},{1,2},{2,3},{3,4},{4,5},{5,6},{6,7},{7,8},{8,9},{9,10},{10,1... | collective-permute-start | bytes 786440 | tf_op jit(solution)/shard_map/while/body/eval_jaxpr/ppermute | solution.py:13
  378.4 9.4 %collective-permute-start = (bf16[128,1024]{1,0:T(8,128)(2,1)S(1)}, bf16[128,1024]{1,0:T(8,128)(2,1)S(1)}, u32[]{:S(2)}, u32[]{:S(2)}) collective-permute-start(bf16[128,1024]{1,0:T(8,128)(2,1)S(1)} %get-tuple-element.321), channel_id=1, source_target_pairs={{0,1},{1,2},{2,3},{3,4},{4,5},{5,6},{6,7},{7,8},{8,9},{9,10},{10,1... | collective-permute-start | bytes 786440 | tf_op jit(solution)/shard_map/while/body/eval_jaxpr/ppermute | solution.py:13
  380.3 10.3 %collective-permute-start.1 = (bf16[128,1024]{1,0:T(8,128)(2,1)}, bf16[128,1024]{1,0:T(8,128)(2,1)S(1)}, u32[]{:S(2)}, u32[]{:S(2)}) collective-permute-start(bf16[128,1024]{1,0:T(8,128)(2,1)} %get-tuple-element.322), channel_id=1, source_target_pairs={{0,1},{1,2},{2,3},{3,4},{4,5},{5,6},{6,7},{7,8},{8,9},{9,10},{10,1... | collective-permute-start | bytes 786440 | tf_op jit(solution)/shard_map/while/body/eval_jaxpr/ppermute | solution.py:13
  393.3 9.2 %collective-permute-start = (bf16[128,1024]{1,0:T(8,128)(2,1)S(1)}, bf16[128,1024]{1,0:T(8,128)(2,1)S(1)}, u32[]{:S(2)}, u32[]{:S(2)}) collective-permute-start(bf16[128,1024]{1,0:T(8,128)(2,1)S(1)} %get-tuple-element.321), channel_id=1, source_target_pairs={{0,1},{1,2},{2,3},{3,4},{4,5},{5,6},{6,7},{7,8},{8,9},{9,10},{10,1... | collective-permute-start | bytes 786440 | tf_op jit(solution)/shard_map/while/body/eval_jaxpr/ppermute | solution.py:13
  395.2 10.1 %collective-permute-start.1 = (bf16[128,1024]{1,0:T(8,128)(2,1)}, bf16[128,1024]{1,0:T(8,128)(2,1)S(1)}, u32[]{:S(2)}, u32[]{:S(2)}) collective-permute-start(bf16[128,1024]{1,0:T(8,128)(2,1)} %get-tuple-element.322), channel_id=1, source_target_pairs={{0,1},{1,2},{2,3},{3,4},{4,5},{5,6},{6,7},{7,8},{8,9},{9,10},{10,1... | collective-permute-start | bytes 786440 | tf_op jit(solution)/shard_map/while/body/eval_jaxpr/ppermute | solution.py:13
  408.1 9.2 %collective-permute-start = (bf16[128,1024]{1,0:T(8,128)(2,1)S(1)}, bf16[128,1024]{1,0:T(8,128)(2,1)S(1)}, u32[]{:S(2)}, u32[]{:S(2)}) collective-permute-start(bf16[128,1024]{1,0:T(8,128)(2,1)S(1)} %get-tuple-element.321), channel_id=1, source_target_pairs={{0,1},{1,2},{2,3},{3,4},{4,5},{5,6},{6,7},{7,8},{8,9},{9,10},{10,1... | collective-permute-start | bytes 786440 | tf_op jit(solution)/shard_map/while/body/eval_jaxpr/ppermute | solution.py:13
  410.0 10.1 %collective-permute-start.1 = (bf16[128,1024]{1,0:T(8,128)(2,1)}, bf16[128,1024]{1,0:T(8,128)(2,1)S(1)}, u32[]{:S(2)}, u32[]{:S(2)}) collective-permute-start(bf16[128,1024]{1,0:T(8,128)(2,1)} %get-tuple-element.322), channel_id=1, source_target_pairs={{0,1},{1,2},{2,3},{3,4},{4,5},{5,6},{6,7},{7,8},{8,9},{9,10},{10,1... | collective-permute-start | bytes 786440 | tf_op jit(solution)/shard_map/while/body/eval_jaxpr/ppermute | solution.py:13
  422.9 9.2 %collective-permute-start = (bf16[128,1024]{1,0:T(8,128)(2,1)S(1)}, bf16[128,1024]{1,0:T(8,128)(2,1)S(1)}, u32[]{:S(2)}, u32[]{:S(2)}) collective-permute-start(bf16[128,1024]{1,0:T(8,128)(2,1)S(1)} %get-tuple-element.321), channel_id=1, source_target_pairs={{0,1},{1,2},{2,3},{3,4},{4,5},{5,6},{6,7},{7,8},{8,9},{9,10},{10,1... | collective-permute-start | bytes 786440 | tf_op jit(solution)/shard_map/while/body/eval_jaxpr/ppermute | solution.py:13
  424.8 10.1 %collective-permute-start.1 = (bf16[128,1024]{1,0:T(8,128)(2,1)}, bf16[128,1024]{1,0:T(8,128)(2,1)S(1)}, u32[]{:S(2)}, u32[]{:S(2)}) collective-permute-start(bf16[128,1024]{1,0:T(8,128)(2,1)} %get-tuple-element.322), channel_id=1, source_target_pairs={{0,1},{1,2},{2,3},{3,4},{4,5},{5,6},{6,7},{7,8},{8,9},{9,10},{10,1... | collective-permute-start | bytes 786440 | tf_op jit(solution)/shard_map/while/body/eval_jaxpr/ppermute | solution.py:13
  437.6 10.2 %collective-permute-start = (bf16[128,1024]{1,0:T(8,128)(2,1)S(1)}, bf16[128,1024]{1,0:T(8,128)(2,1)S(1)}, u32[]{:S(2)}, u32[]{:S(2)}) collective-permute-start(bf16[128,1024]{1,0:T(8,128)(2,1)S(1)} %get-tuple-element.321), channel_id=1, source_target_pairs={{0,1},{1,2},{2,3},{3,4},{4,5},{5,6},{6,7},{7,8},{8,9},{9,10},{10,1... | collective-permute-start | bytes 786440 | tf_op jit(solution)/shard_map/while/body/eval_jaxpr/ppermute | solution.py:13
  439.5 11.1 %collective-permute-start.1 = (bf16[128,1024]{1,0:T(8,128)(2,1)}, bf16[128,1024]{1,0:T(8,128)(2,1)S(1)}, u32[]{:S(2)}, u32[]{:S(2)}) collective-permute-start(bf16[128,1024]{1,0:T(8,128)(2,1)} %get-tuple-element.322), channel_id=1, source_target_pairs={{0,1},{1,2},{2,3},{3,4},{4,5},{5,6},{6,7},{7,8},{8,9},{9,10},{10,1... | collective-permute-start | bytes 786440 | tf_op jit(solution)/shard_map/while/body/eval_jaxpr/ppermute | solution.py:13
  453.4 11.2 %collective-permute-start = (bf16[128,1024]{1,0:T(8,128)(2,1)S(1)}, bf16[128,1024]{1,0:T(8,128)(2,1)S(1)}, u32[]{:S(2)}, u32[]{:S(2)}) collective-permute-start(bf16[128,1024]{1,0:T(8,128)(2,1)S(1)} %get-tuple-element.321), channel_id=1, source_target_pairs={{0,1},{1,2},{2,3},{3,4},{4,5},{5,6},{6,7},{7,8},{8,9},{9,10},{10,1... | collective-permute-start | bytes 786440 | tf_op jit(solution)/shard_map/while/body/eval_jaxpr/ppermute | solution.py:13
  455.3 12.1 %collective-permute-start.1 = (bf16[128,1024]{1,0:T(8,128)(2,1)}, bf16[128,1024]{1,0:T(8,128)(2,1)S(1)}, u32[]{:S(2)}, u32[]{:S(2)}) collective-permute-start(bf16[128,1024]{1,0:T(8,128)(2,1)} %get-tuple-element.322), channel_id=1, source_target_pairs={{0,1},{1,2},{2,3},{3,4},{4,5},{5,6},{6,7},{7,8},{8,9},{9,10},{10,1... | collective-permute-start | bytes 786440 | tf_op jit(solution)/shard_map/while/body/eval_jaxpr/ppermute | solution.py:13
  470.2 12.4 %collective-permute-start = (bf16[128,1024]{1,0:T(8,128)(2,1)S(1)}, bf16[128,1024]{1,0:T(8,128)(2,1)S(1)}, u32[]{:S(2)}, u32[]{:S(2)}) collective-permute-start(bf16[128,1024]{1,0:T(8,128)(2,1)S(1)} %get-tuple-element.321), channel_id=1, source_target_pairs={{0,1},{1,2},{2,3},{3,4},{4,5},{5,6},{6,7},{7,8},{8,9},{9,10},{10,1... | collective-permute-start | bytes 786440 | tf_op jit(solution)/shard_map/while/body/eval_jaxpr/ppermute | solution.py:13
  472.1 13.2 %collective-permute-start.1 = (bf16[128,1024]{1,0:T(8,128)(2,1)}, bf16[128,1024]{1,0:T(8,128)(2,1)S(1)}, u32[]{:S(2)}, u32[]{:S(2)}) collective-permute-start(bf16[128,1024]{1,0:T(8,128)(2,1)} %get-tuple-element.322), channel_id=1, source_target_pairs={{0,1},{1,2},{2,3},{3,4},{4,5},{5,6},{6,7},{7,8},{8,9},{9,10},{10,1... | collective-permute-start | bytes 786440 | tf_op jit(solution)/shard_map/while/body/eval_jaxpr/ppermute | solution.py:13
  488.0 12.4 %collective-permute-start = (bf16[128,1024]{1,0:T(8,128)(2,1)S(1)}, bf16[128,1024]{1,0:T(8,128)(2,1)S(1)}, u32[]{:S(2)}, u32[]{:S(2)}) collective-permute-start(bf16[128,1024]{1,0:T(8,128)(2,1)S(1)} %get-tuple-element.321), channel_id=1, source_target_pairs={{0,1},{1,2},{2,3},{3,4},{4,5},{5,6},{6,7},{7,8},{8,9},{9,10},{10,1... | collective-permute-start | bytes 786440 | tf_op jit(solution)/shard_map/while/body/eval_jaxpr/ppermute | solution.py:13
  489.9 14.3 %collective-permute-start.1 = (bf16[128,1024]{1,0:T(8,128)(2,1)}, bf16[128,1024]{1,0:T(8,128)(2,1)S(1)}, u32[]{:S(2)}, u32[]{:S(2)}) collective-permute-start(bf16[128,1024]{1,0:T(8,128)(2,1)} %get-tuple-element.322), channel_id=1, source_target_pairs={{0,1},{1,2},{2,3},{3,4},{4,5},{5,6},{6,7},{7,8},{8,9},{9,10},{10,1... | collective-permute-start | bytes 786440 | tf_op jit(solution)/shard_map/while/body/eval_jaxpr/ppermute | solution.py:13
  507.0 12.2 %collective-permute-start = (bf16[128,1024]{1,0:T(8,128)(2,1)S(1)}, bf16[128,1024]{1,0:T(8,128)(2,1)S(1)}, u32[]{:S(2)}, u32[]{:S(2)}) collective-permute-start(bf16[128,1024]{1,0:T(8,128)(2,1)S(1)} %get-tuple-element.321), channel_id=1, source_target_pairs={{0,1},{1,2},{2,3},{3,4},{4,5},{5,6},{6,7},{7,8},{8,9},{9,10},{10,1... | collective-permute-start | bytes 786440 | tf_op jit(solution)/shard_map/while/body/eval_jaxpr/ppermute | solution.py:13
  508.9 15.4 %collective-permute-start.1 = (bf16[128,1024]{1,0:T(8,128)(2,1)}, bf16[128,1024]{1,0:T(8,128)(2,1)S(1)}, u32[]{:S(2)}, u32[]{:S(2)}) collective-permute-start(bf16[128,1024]{1,0:T(8,128)(2,1)} %get-tuple-element.322), channel_id=1, source_target_pairs={{0,1},{1,2},{2,3},{3,4},{4,5},{5,6},{6,7},{7,8},{8,9},{9,10},{10,1... | collective-permute-start | bytes 786440 | tf_op jit(solution)/shard_map/while/body/eval_jaxpr/ppermute | solution.py:13
  527.1 11.9 %collective-permute-start.3 = (bf16[128,1024]{1,0:T(8,128)(2,1)}, bf16[128,1024]{1,0:T(8,128)(2,1)S(1)}, u32[]{:S(2)}, u32[]{:S(2)}) collective-permute-start(bf16[128,1024]{1,0:T(8,128)(2,1)} %get-tuple-element.228), channel_id=1, source_target_pairs={{0,1},{1,2},{2,3},{3,4},{4,5},{5,6},{6,7},{7,8},{8,9},{9,10},{10,1... | collective-permute-start | bytes 786440 | tf_op jit(solution)/shard_map/ppermute | solution.py:13
  (1 other events, 5.8 us)
Sparse Core Ops, SparseCore 0:
  539.9 176.4 all-reduce.1
where the time goes:
time: 728 us; the launch traced here: 725 us
  waiting for transfers between devices  459 us (63%)
  starting transfers between devices  145 us (20%)
  matrix products  95.9 us (13%)
  between operations  14.1 us (2%)
  other arithmetic  7.82 us (1%)
    ppermute x62, waiting for transfers between devices, passed_along(): lax.ppermute(array, axis, [(i, (i + by) % peers) for i in range(peers)])  283 us
    psum x1, waiting for transfers between devices, body(): summed = lax.psum(finished.astype(jnp.bfloat16), 'dp').astype(jnp.float32)  176 us
    ppermute x62, starting transfers between devices, passed_along(): lax.ppermute(array, axis, [(i, (i + by) % peers) for i in range(peers)])  145 us
    dot_general x32, matrix products, visit(): lax.dot_general(out_grad, weight, (((1,), (1,)), ((), ())), preferred_ele...  57.1 us
    dot_general x32, matrix products, visit(): lax.dot_general(hidden_part, out_grad, (((0,), (0,)), ((), ())), preferre...  30.2 us
  transfers between devices with their start and end apart: 63, of which 63 were waited for; matrix products, arithmetic and copies ran while one was open for 3% of the time, Pallas kernels for 0%

commit v1 on v0

--- a/solution.py
+++ b/solution.py
@@ -1,3 +1,4 @@
+import functools
 import math
 import jax
 import jax.numpy as jnp
@@ -6,6 +7,14 @@
 
 SQRT_TWO_PI = 0.7978845608028654
 CUBIC = 0.044715
+
+
+def _push_threads(frame, device_axis):
+    z2 = lax.all_gather(frame, axis_name=device_axis).sum(axis=0)
+    return z2
+
+
+cut_stacks_all = functools.partial(_push_threads, device_axis="dp")
 
 
 def passed_along(array, axis, by):
@@ -86,7 +95,7 @@
     )
     finished = finish_partial(pass_grad(partial_value), own_term)
     out_total, grad_buffer = carried
-    summed = lax.psum(finished.astype(jnp.bfloat16), "dp").astype(jnp.float32)
+    summed = cut_stacks_all(finished.astype(jnp.bfloat16)).astype(jnp.float32)
     token_count = row_count * cycle_size * lax.axis_size("dp")
     return (out_total.astype(jnp.bfloat16), grad_buffer, summed / math.sqrt(token_count))
 

time: 728 us -> 648 us (0.89)
  waiting for transfers between devices: 459 us -> 377 us
    psum x1 -> x0, waiting for transfers between devices: 176 us -> none  [body(): summed = lax.psum(finished.astype(jnp.bfloat16), 'dp').astype(jnp.float32)]
    all_gather x0 -> x1, waiting for transfers between devices: none -> 94.2 us  [_push_threads(): z2 = lax.all_gather(frame, axis_name=device_axis).sum(axis=0)]
where the time goes in v1:
time: 648 us; the launch traced here: 646 us
  waiting for transfers between devices  377 us (58%)
  starting transfers between devices  145 us (22%)
  matrix products  95.9 us (15%)
  between operations  14.1 us (2%)
  other arithmetic  9.99 us (2%)
    ppermute x62, waiting for transfers between devices, passed_along(): lax.ppermute(array, axis, [(i, (i + by) % peers) for i in range(peers)])  283 us
    ppermute x62, starting transfers between devices, passed_along(): lax.ppermute(array, axis, [(i, (i + by) % peers) for i in range(peers)])  145 us
    all_gather x1, waiting for transfers between devices, _push_threads(): z2 = lax.all_gather(frame, axis_name=device_axis).sum(axis=0)  94.2 us
    dot_general x32, matrix products, visit(): lax.dot_general(out_grad, weight, (((1,), (1,)), ((), ())), preferred_ele...  57.1 us
    dot_general x32, matrix products, visit(): lax.dot_general(hidden_part, out_grad, (((0,), (0,)), ((), ())), preferre...  30.2 us
  transfers between devices with their start and end apart: 63, of which 63 were waited for; matrix products, arithmetic and copies ran while one was open for 3% of the time, Pallas kernels for 0%

profile of v1, /device:TPU:1, one launch (start us, length us, event | category | flops | bytes accessed | tf_op | source)
XLA Modules:
  0.0 645.6 jit_solution(17437837454044028708)
XLA Ops:
  7.2 4.4 collective-permute-start.2
  11.6 4.5 fusion.14
  20.4 5.9 collective-permute-done.2
  28.4 498.7 %while.21 = (s32[]{:T(128)}, bf16[128,1024]{1,0:T(8,128)(2,1)S(1)}, bf16[128,1024]{1,0:T(8,128)(2,1)}, f32[192,1024]{1,0:T(8,128)S(1)}, bf16[192,4096]{1,0:T(8,1...) while((s32[]{:T(128)}, bf16[128,1024]{1,0:T(8,128)(2,1)S(1)}, ...), condition=%wide.region_1.2_spmd, body=%wide.region_0.1_spmd.sunk | while | flops 151633936 | bytes 6275492 | solution.py:93
  32.3 6.7 %collective-permute-done = bf16[128,1024]{1,0:T(8,128)(2,1)S(1)} collective-permute-done((bf16[128,1024]{1,0:T(8,128)(2,1)S(1)}, bf16[128,1024]{1,0:T(8,128)(2,1)S(1)}, u32[]{:S(2)}, u32[]{:S(2)}) %collective-permute-start) | collective-permute-done | bytes 262176 | tf_op jit(solution)/shard_map/while/body/eval_jaxpr/ppermute | solution.py:22
  39.3 5.3 collective-permute-done.1
  51.2 5.8 collective-permute-done
  57.3 5.3 collective-permute-done.1
  69.2 5.3 collective-permute-done
  74.9 4.8 collective-permute-done.1
  86.3 5.3 collective-permute-done
  91.9 3.9 collective-permute-done.1
  102.4 5.3 collective-permute-done
  108.1 3.0 collective-permute-done.1
  117.7 5.3 collective-permute-done
  123.3 2.5 collective-permute-done.1
  132.5 5.3 collective-permute-done
  138.1 2.5 collective-permute-done.1
  145.3 3.0 collective-permute-start.1
  148.3 4.2 collective-permute-done
  158.1 2.7 collective-permute-start
  160.9 4.0 collective-permute-start.1
  167.6 2.7 collective-permute-done.1
  173.1 3.9 collective-permute-start
  177.0 4.4 collective-permute-start.1
  183.0 3.4 collective-permute-done.1
  189.1 5.1 collective-permute-start
  194.2 4.0 collective-permute-start.1
  199.3 4.4 collective-permute-done.1
  206.4 4.5 collective-permute-start
  211.0 4.0 collective-permute-start.1
  215.9 4.5 collective-permute-done.1
  223.2 2.9 collective-permute-start
  226.1 4.0 collective-permute-start.1
  232.7 2.8 collective-permute-done.1
  240.2 4.0 collective-permute-start.1
  244.2 4.8 collective-permute-done
  258.5 8.2 %collective-permute-done = bf16[128,1024]{1,0:T(8,128)(2,1)S(1)} collective-permute-done((bf16[128,1024]{1,0:T(8,128)(2,1)S(1)}, bf16[128,1024]{1,0:T(8,128)(2,1)S(1)}, u32[]{:S(2)}, u32[]{:S(2)}) %collective-permute-start) | collective-permute-done | bytes 262176 | tf_op jit(solution)/shard_map/while/body/eval_jaxpr/ppermute | solution.py:22
  267.0 5.3 collective-permute-done.1
  278.9 7.3 %collective-permute-done = bf16[128,1024]{1,0:T(8,128)(2,1)S(1)} collective-permute-done((bf16[128,1024]{1,0:T(8,128)(2,1)S(1)}, bf16[128,1024]{1,0:T(8,128)(2,1)S(1)}, u32[]{:S(2)}, u32[]{:S(2)}) %collective-permute-start) | collective-permute-done | bytes 262176 | tf_op jit(solution)/shard_map/while/body/eval_jaxpr/ppermute | solution.py:22
  286.5 5.3 collective-permute-done.1
  298.5 6.4 collective-permute-done
  305.2 5.3 collective-permute-done.1
  317.1 5.3 collective-permute-done
  322.7 5.5 collective-permute-done.1
  334.8 5.3 collective-permute-done
  340.5 4.5 collective-permute-done.1
  351.6 5.3 collective-permute-done
  357.3 3.6 collective-permute-done.1
  367.5 5.3 collective-permute-done
  382.3 5.5 collective-permute-done
  397.2 5.3 collective-permute-done
  412.0 5.3 collective-permute-done
  426.7 5.3 collective-permute-done
  441.5 6.3 collective-permute-done
  457.5 7.1 %collective-permute-done = bf16[128,1024]{1,0:T(8,128)(2,1)S(1)} collective-permute-done((bf16[128,1024]{1,0:T(8,128)(2,1)S(1)}, bf16[128,1024]{1,0:T(8,128)(2,1)S(1)}, u32[]{:S(2)}, u32[]{:S(2)}) %collective-permute-start) | collective-permute-done | bytes 262176 | tf_op jit(solution)/shard_map/while/body/eval_jaxpr/ppermute | solution.py:22
  474.0 8.5 %collective-permute-done = bf16[128,1024]{1,0:T(8,128)(2,1)S(1)} collective-permute-done((bf16[128,1024]{1,0:T(8,128)(2,1)S(1)}, bf16[128,1024]{1,0:T(8,128)(2,1)S(1)}, u32[]{:S(2)}, u32[]{:S(2)}) %collective-permute-start) | collective-permute-done | bytes 262176 | tf_op jit(solution)/shard_map/while/body/eval_jaxpr/ppermute | solution.py:22
  491.9 8.5 %collective-permute-done = bf16[128,1024]{1,0:T(8,128)(2,1)S(1)} collective-permute-done((bf16[128,1024]{1,0:T(8,128)(2,1)S(1)}, bf16[128,1024]{1,0:T(8,128)(2,1)S(1)}, u32[]{:S(2)}, u32[]{:S(2)}) %collective-permute-start) | collective-permute-done | bytes 262176 | tf_op jit(solution)/shard_map/while/body/eval_jaxpr/ppermute | solution.py:22
  500.7 3.5 collective-permute-done.1
  510.9 8.3 %collective-permute-done = bf16[128,1024]{1,0:T(8,128)(2,1)S(1)} collective-permute-done((bf16[128,1024]{1,0:T(8,128)(2,1)S(1)}, bf16[128,1024]{1,0:T(8,128)(2,1)S(1)}, u32[]{:S(2)}, u32[]{:S(2)}) %collective-permute-start) | collective-permute-done | bytes 262176 | tf_op jit(solution)/shard_map/while/body/eval_jaxpr/ppermute | solution.py:22
  519.5 4.8 collective-permute-done.1
  529.2 9.8 %collective-permute-done.3 = bf16[128,1024]{1,0:T(8,128)(2,1)S(1)} collective-permute-done((bf16[128,1024]{1,0:T(8,128)(2,1)}, bf16[128,1024]{1,0:T(8,128)(2,1)S(1)}, u32[]{:S(2)}, u32[]{:S(2)}) %collective-permute-start.3) | collective-permute-done | bytes 262176 | tf_op jit(solution)/shard_map/ppermute | solution.py:22
  540.6 94.2 %all-gather.3.cloned.1.call-done = bf16[2048,1024]{1,0:T(8,128)(2,1)} async-done(((bf16[128,1024]{1,0:T(8,128)(2,1)}), bf16[2048,1024]{1,0:T(8,128)(2,1)}) %all-gather.3.cloned.1.call-update) | async-done | bytes 4194320 | tf_op jit(solution)/shard_map/all_gather | solution.py:13
  634.8 3.1 reduce_sum.12
  (200 shorter events, 226.7 us)
Async XLA Ops:
  7.2 627.6 %all-gather.3.cloned.1.call-start = ((), (), s32[]{:S(2)}) async-start(), calls=%async_computation | async-start | bytes 4456448 | tf_op jit(solution)/shard_map/all_gather | solution.py:13
  7.2 19.1 %collective-permute-start.2 = (bf16[128,1024]{1,0:T(8,128)(2,1)}, bf16[128,1024]{1,0:T(8,128)(2,1)S(1)}, u32[]{:S(2)}, u32[]{:S(2)}) collective-permute-start(bf16[128,1024]{1,0:T(8,128)(2,1)} %param.7), channel_id=1, source_target_pairs={{0,1},{1,2},{2,3},{3,4},{4,5},{5,6},{6,7},{7,8},{8,9},{9,10},{10,1... | collective-permute-start | bytes 786440 | tf_op jit(solution)/shard_map/ppermute | solution.py:22
  11.6 5.8 copy-start
  28.4 10.6 %collective-permute-start = (bf16[128,1024]{1,0:T(8,128)(2,1)S(1)}, bf16[128,1024]{1,0:T(8,128)(2,1)S(1)}, u32[]{:S(2)}, u32[]{:S(2)}) collective-permute-start(bf16[128,1024]{1,0:T(8,128)(2,1)S(1)} %get-tuple-element.321), channel_id=1, source_target_pairs={{0,1},{1,2},{2,3},{3,4},{4,5},{5,6},{6,7},{7,8},{8,9},{9,10},{10,1... | collective-permute-start | bytes 786440 | tf_op jit(solution)/shard_map/while/body/eval_jaxpr/ppermute | solution.py:22
  30.3 14.3 %collective-permute-start.1 = (bf16[128,1024]{1,0:T(8,128)(2,1)}, bf16[128,1024]{1,0:T(8,128)(2,1)S(1)}, u32[]{:S(2)}, u32[]{:S(2)}) collective-permute-start(bf16[128,1024]{1,0:T(8,128)(2,1)} %get-tuple-element.322), channel_id=1, source_target_pairs={{0,1},{1,2},{2,3},{3,4},{4,5},{5,6},{6,7},{7,8},{8,9},{9,10},{10,1... | collective-permute-start | bytes 786440 | tf_op jit(solution)/shard_map/while/body/eval_jaxpr/ppermute | solution.py:22
  47.3 9.6 %collective-permute-start = (bf16[128,1024]{1,0:T(8,128)(2,1)S(1)}, bf16[128,1024]{1,0:T(8,128)(2,1)S(1)}, u32[]{:S(2)}, u32[]{:S(2)}) collective-permute-start(bf16[128,1024]{1,0:T(8,128)(2,1)S(1)} %get-tuple-element.321), channel_id=1, source_target_pairs={{0,1},{1,2},{2,3},{3,4},{4,5},{5,6},{6,7},{7,8},{8,9},{9,10},{10,1... | collective-permute-start | bytes 786440 | tf_op jit(solution)/shard_map/while/body/eval_jaxpr/ppermute | solution.py:22
  49.3 13.3 %collective-permute-start.1 = (bf16[128,1024]{1,0:T(8,128)(2,1)}, bf16[128,1024]{1,0:T(8,128)(2,1)S(1)}, u32[]{:S(2)}, u32[]{:S(2)}) collective-permute-start(bf16[128,1024]{1,0:T(8,128)(2,1)} %get-tuple-element.322), channel_id=1, source_target_pairs={{0,1},{1,2},{2,3},{3,4},{4,5},{5,6},{6,7},{7,8},{8,9},{9,10},{10,1... | collective-permute-start | bytes 786440 | tf_op jit(solution)/shard_map/while/body/eval_jaxpr/ppermute | solution.py:22
  65.3 9.2 %collective-permute-start = (bf16[128,1024]{1,0:T(8,128)(2,1)S(1)}, bf16[128,1024]{1,0:T(8,128)(2,1)S(1)}, u32[]{:S(2)}, u32[]{:S(2)}) collective-permute-start(bf16[128,1024]{1,0:T(8,128)(2,1)S(1)} %get-tuple-element.321), channel_id=1, source_target_pairs={{0,1},{1,2},{2,3},{3,4},{4,5},{5,6},{6,7},{7,8},{8,9},{9,10},{10,1... | collective-permute-start | bytes 786440 | tf_op jit(solution)/shard_map/while/body/eval_jaxpr/ppermute | solution.py:22
  67.3 12.4 %collective-permute-start.1 = (bf16[128,1024]{1,0:T(8,128)(2,1)}, bf16[128,1024]{1,0:T(8,128)(2,1)S(1)}, u32[]{:S(2)}, u32[]{:S(2)}) collective-permute-start(bf16[128,1024]{1,0:T(8,128)(2,1)} %get-tuple-element.322), channel_id=1, source_target_pairs={{0,1},{1,2},{2,3},{3,4},{4,5},{5,6},{6,7},{7,8},{8,9},{9,10},{10,1... | collective-permute-start | bytes 786440 | tf_op jit(solution)/shard_map/while/body/eval_jaxpr/ppermute | solution.py:22
  82.4 9.2 %collective-permute-start = (bf16[128,1024]{1,0:T(8,128)(2,1)S(1)}, bf16[128,1024]{1,0:T(8,128)(2,1)S(1)}, u32[]{:S(2)}, u32[]{:S(2)}) collective-permute-start(bf16[128,1024]{1,0:T(8,128)(2,1)S(1)} %get-tuple-element.321), channel_id=1, source_target_pairs={{0,1},{1,2},{2,3},{3,4},{4,5},{5,6},{6,7},{7,8},{8,9},{9,10},{10,1... | collective-permute-start | bytes 786440 | tf_op jit(solution)/shard_map/while/body/eval_jaxpr/ppermute | solution.py:22
  84.3 11.5 %collective-permute-start.1 = (bf16[128,1024]{1,0:T(8,128)(2,1)}, bf16[128,1024]{1,0:T(8,128)(2,1)S(1)}, u32[]{:S(2)}, u32[]{:S(2)}) collective-permute-start(bf16[128,1024]{1,0:T(8,128)(2,1)} %get-tuple-element.322), channel_id=1, source_target_pairs={{0,1},{1,2},{2,3},{3,4},{4,5},{5,6},{6,7},{7,8},{8,9},{9,10},{10,1... | collective-permute-start | bytes 786440 | tf_op jit(solution)/shard_map/while/body/eval_jaxpr/ppermute | solution.py:22
  98.6 9.2 %collective-permute-start = (bf16[128,1024]{1,0:T(8,128)(2,1)S(1)}, bf16[128,1024]{1,0:T(8,128)(2,1)S(1)}, u32[]{:S(2)}, u32[]{:S(2)}) collective-permute-start(bf16[128,1024]{1,0:T(8,128)(2,1)S(1)} %get-tuple-element.321), channel_id=1, source_target_pairs={{0,1},{1,2},{2,3},{3,4},{4,5},{5,6},{6,7},{7,8},{8,9},{9,10},{10,1... | collective-permute-start | bytes 786440 | tf_op jit(solution)/shard_map/while/body/eval_jaxpr/ppermute | solution.py:22
  100.5 10.6 %collective-permute-start.1 = (bf16[128,1024]{1,0:T(8,128)(2,1)}, bf16[128,1024]{1,0:T(8,128)(2,1)S(1)}, u32[]{:S(2)}, u32[]{:S(2)}) collective-permute-start(bf16[128,1024]{1,0:T(8,128)(2,1)} %get-tuple-element.322), channel_id=1, source_target_pairs={{0,1},{1,2},{2,3},{3,4},{4,5},{5,6},{6,7},{7,8},{8,9},{9,10},{10,1... | collective-permute-start | bytes 786440 | tf_op jit(solution)/shard_map/while/body/eval_jaxpr/ppermute | solution.py:22
  113.8 9.2 %collective-permute-start = (bf16[128,1024]{1,0:T(8,128)(2,1)S(1)}, bf16[128,1024]{1,0:T(8,128)(2,1)S(1)}, u32[]{:S(2)}, u32[]{:S(2)}) collective-permute-start(bf16[128,1024]{1,0:T(8,128)(2,1)S(1)} %get-tuple-element.321), channel_id=1, source_target_pairs={{0,1},{1,2},{2,3},{3,4},{4,5},{5,6},{6,7},{7,8},{8,9},{9,10},{10,1... | collective-permute-start | bytes 786440 | tf_op jit(solution)/shard_map/while/body/eval_jaxpr/ppermute | solution.py:22
  115.7 10.1 %collective-permute-start.1 = (bf16[128,1024]{1,0:T(8,128)(2,1)}, bf16[128,1024]{1,0:T(8,128)(2,1)S(1)}, u32[]{:S(2)}, u32[]{:S(2)}) collective-permute-start(bf16[128,1024]{1,0:T(8,128)(2,1)} %get-tuple-element.322), channel_id=1, source_target_pairs={{0,1},{1,2},{2,3},{3,4},{4,5},{5,6},{6,7},{7,8},{8,9},{9,10},{10,1... | collective-permute-start | bytes 786440 | tf_op jit(solution)/shard_map/while/body/eval_jaxpr/ppermute | solution.py:22
  128.6 9.2 %collective-permute-start = (bf16[128,1024]{1,0:T(8,128)(2,1)S(1)}, bf16[128,1024]{1,0:T(8,128)(2,1)S(1)}, u32[]{:S(2)}, u32[]{:S(2)}) collective-permute-start(bf16[128,1024]{1,0:T(8,128)(2,1)S(1)} %get-tuple-element.321), channel_id=1, source_target_pairs={{0,1},{1,2},{2,3},{3,4},{4,5},{5,6},{6,7},{7,8},{8,9},{9,10},{10,1... | collective-permute-start | bytes 786440 | tf_op jit(solution)/shard_map/while/body/eval_jaxpr/ppermute | solution.py:22
  130.5 10.1 %collective-permute-start.1 = (bf16[128,1024]{1,0:T(8,128)(2,1)}, bf16[128,1024]{1,0:T(8,128)(2,1)S(1)}, u32[]{:S(2)}, u32[]{:S(2)}) collective-permute-start(bf16[128,1024]{1,0:T(8,128)(2,1)} %get-tuple-element.322), channel_id=1, source_target_pairs={{0,1},{1,2},{2,3},{3,4},{4,5},{5,6},{6,7},{7,8},{8,9},{9,10},{10,1... | collective-permute-start | bytes 786440 | tf_op jit(solution)/shard_map/while/body/eval_jaxpr/ppermute | solution.py:22
  143.4 9.2 %collective-permute-start = (bf16[128,1024]{1,0:T(8,128)(2,1)S(1)}, bf16[128,1024]{1,0:T(8,128)(2,1)S(1)}, u32[]{:S(2)}, u32[]{:S(2)}) collective-permute-start(bf16[128,1024]{1,0:T(8,128)(2,1)S(1)} %get-tuple-element.321), channel_id=1, source_target_pairs={{0,1},{1,2},{2,3},{3,4},{4,5},{5,6},{6,7},{7,8},{8,9},{9,10},{10,1... | collective-permute-start | bytes 786440 | tf_op jit(solution)/shard_map/while/body/eval_jaxpr/ppermute | solution.py:22
  145.3 10.1 %collective-permute-start.1 = (bf16[128,1024]{1,0:T(8,128)(2,1)}, bf16[128,1024]{1,0:T(8,128)(2,1)S(1)}, u32[]{:S(2)}, u32[]{:S(2)}) collective-permute-start(bf16[128,1024]{1,0:T(8,128)(2,1)} %get-tuple-element.322), channel_id=1, source_target_pairs={{0,1},{1,2},{2,3},{3,4},{4,5},{5,6},{6,7},{7,8},{8,9},{9,10},{10,1... | collective-permute-start | bytes 786440 | tf_op jit(solution)/shard_map/while/body/eval_jaxpr/ppermute | solution.py:22
  158.1 9.2 %collective-permute-start = (bf16[128,1024]{1,0:T(8,128)(2,1)S(1)}, bf16[128,1024]{1,0:T(8,128)(2,1)S(1)}, u32[]{:S(2)}, u32[]{:S(2)}) collective-permute-start(bf16[128,1024]{1,0:T(8,128)(2,1)S(1)} %get-tuple-element.321), channel_id=1, source_target_pairs={{0,1},{1,2},{2,3},{3,4},{4,5},{5,6},{6,7},{7,8},{8,9},{9,10},{10,1... | collective-permute-start | bytes 786440 | tf_op jit(solution)/shard_map/while/body/eval_jaxpr/ppermute | solution.py:22
  160.9 9.4 %collective-permute-start.1 = (bf16[128,1024]{1,0:T(8,128)(2,1)}, bf16[128,1024]{1,0:T(8,128)(2,1)S(1)}, u32[]{:S(2)}, u32[]{:S(2)}) collective-permute-start(bf16[128,1024]{1,0:T(8,128)(2,1)} %get-tuple-element.322), channel_id=1, source_target_pairs={{0,1},{1,2},{2,3},{3,4},{4,5},{5,6},{6,7},{7,8},{8,9},{9,10},{10,1... | collective-permute-start | bytes 786440 | tf_op jit(solution)/shard_map/while/body/eval_jaxpr/ppermute | solution.py:22
  173.1 9.6 %collective-permute-start = (bf16[128,1024]{1,0:T(8,128)(2,1)S(1)}, bf16[128,1024]{1,0:T(8,128)(2,1)S(1)}, u32[]{:S(2)}, u32[]{:S(2)}) collective-permute-start(bf16[128,1024]{1,0:T(8,128)(2,1)S(1)} %get-tuple-element.321), channel_id=1, source_target_pairs={{0,1},{1,2},{2,3},{3,4},{4,5},{5,6},{6,7},{7,8},{8,9},{9,10},{10,1... | collective-permute-start | bytes 786440 | tf_op jit(solution)/shard_map/while/body/eval_jaxpr/ppermute | solution.py:22
  177.0 9.4 %collective-permute-start.1 = (bf16[128,1024]{1,0:T(8,128)(2,1)}, bf16[128,1024]{1,0:T(8,128)(2,1)S(1)}, u32[]{:S(2)}, u32[]{:S(2)}) collective-permute-start(bf16[128,1024]{1,0:T(8,128)(2,1)} %get-tuple-element.322), channel_id=1, source_target_pairs={{0,1},{1,2},{2,3},{3,4},{4,5},{5,6},{6,7},{7,8},{8,9},{9,10},{10,1... | collective-permute-start | bytes 786440 | tf_op jit(solution)/shard_map/while/body/eval_jaxpr/ppermute | solution.py:22
  189.1 9.9 %collective-permute-start = (bf16[128,1024]{1,0:T(8,128)(2,1)S(1)}, bf16[128,1024]{1,0:T(8,128)(2,1)S(1)}, u32[]{:S(2)}, u32[]{:S(2)}) collective-permute-start(bf16[128,1024]{1,0:T(8,128)(2,1)S(1)} %get-tuple-element.321), channel_id=1, source_target_pairs={{0,1},{1,2},{2,3},{3,4},{4,5},{5,6},{6,7},{7,8},{8,9},{9,10},{10,1... | collective-permute-start | bytes 786440 | tf_op jit(solution)/shard_map/while/body/eval_jaxpr/ppermute | solution.py:22
  194.2 9.4 %collective-permute-start.1 = (bf16[128,1024]{1,0:T(8,128)(2,1)}, bf16[128,1024]{1,0:T(8,128)(2,1)S(1)}, u32[]{:S(2)}, u32[]{:S(2)}) collective-permute-start(bf16[128,1024]{1,0:T(8,128)(2,1)} %get-tuple-element.322), channel_id=1, source_target_pairs={{0,1},{1,2},{2,3},{3,4},{4,5},{5,6},{6,7},{7,8},{8,9},{9,10},{10,1... | collective-permute-start | bytes 786440 | tf_op jit(solution)/shard_map/while/body/eval_jaxpr/ppermute | solution.py:22
  206.4 9.2 %collective-permute-start = (bf16[128,1024]{1,0:T(8,128)(2,1)S(1)}, bf16[128,1024]{1,0:T(8,128)(2,1)S(1)}, u32[]{:S(2)}, u32[]{:S(2)}) collective-permute-start(bf16[128,1024]{1,0:T(8,128)(2,1)S(1)} %get-tuple-element.321), channel_id=1, source_target_pairs={{0,1},{1,2},{2,3},{3,4},{4,5},{5,6},{6,7},{7,8},{8,9},{9,10},{10,1... | collective-permute-start | bytes 786440 | tf_op jit(solution)/shard_map/while/body/eval_jaxpr/ppermute | solution.py:22
  211.0 9.4 %collective-permute-start.1 = (bf16[128,1024]{1,0:T(8,128)(2,1)}, bf16[128,1024]{1,0:T(8,128)(2,1)S(1)}, u32[]{:S(2)}, u32[]{:S(2)}) collective-permute-start(bf16[128,1024]{1,0:T(8,128)(2,1)} %get-tuple-element.322), channel_id=1, source_target_pairs={{0,1},{1,2},{2,3},{3,4},{4,5},{5,6},{6,7},{7,8},{8,9},{9,10},{10,1... | collective-permute-start | bytes 786440 | tf_op jit(solution)/shard_map/while/body/eval_jaxpr/ppermute | solution.py:22
  223.2 9.2 %collective-permute-start = (bf16[128,1024]{1,0:T(8,128)(2,1)S(1)}, bf16[128,1024]{1,0:T(8,128)(2,1)S(1)}, u32[]{:S(2)}, u32[]{:S(2)}) collective-permute-start(bf16[128,1024]{1,0:T(8,128)(2,1)S(1)} %get-tuple-element.321), channel_id=1, source_target_pairs={{0,1},{1,2},{2,3},{3,4},{4,5},{5,6},{6,7},{7,8},{8,9},{9,10},{10,1... | collective-permute-start | bytes 786440 | tf_op jit(solution)/shard_map/while/body/eval_jaxpr/ppermute | solution.py:22
  226.1 9.4 %collective-permute-start.1 = (bf16[128,1024]{1,0:T(8,128)(2,1)}, bf16[128,1024]{1,0:T(8,128)(2,1)S(1)}, u32[]{:S(2)}, u32[]{:S(2)}) collective-permute-start(bf16[128,1024]{1,0:T(8,128)(2,1)} %get-tuple-element.322), channel_id=1, source_target_pairs={{0,1},{1,2},{2,3},{3,4},{4,5},{5,6},{6,7},{7,8},{8,9},{9,10},{10,1... | collective-permute-start | bytes 786440 | tf_op jit(solution)/shard_map/while/body/eval_jaxpr/ppermute | solution.py:22
  238.2 10.8 %collective-permute-start = (bf16[128,1024]{1,0:T(8,128)(2,1)S(1)}, bf16[128,1024]{1,0:T(8,128)(2,1)S(1)}, u32[]{:S(2)}, u32[]{:S(2)}) collective-permute-start(bf16[128,1024]{1,0:T(8,128)(2,1)S(1)} %get-tuple-element.321), channel_id=1, source_target_pairs={{0,1},{1,2},{2,3},{3,4},{4,5},{5,6},{6,7},{7,8},{8,9},{9,10},{10,1... | collective-permute-start | bytes 786440 | tf_op jit(solution)/shard_map/while/body/eval_jaxpr/ppermute | solution.py:22
  240.2 11.6 %collective-permute-start.1 = (bf16[128,1024]{1,0:T(8,128)(2,1)}, bf16[128,1024]{1,0:T(8,128)(2,1)S(1)}, u32[]{:S(2)}, u32[]{:S(2)}) collective-permute-start(bf16[128,1024]{1,0:T(8,128)(2,1)} %get-tuple-element.322), channel_id=1, source_target_pairs={{0,1},{1,2},{2,3},{3,4},{4,5},{5,6},{6,7},{7,8},{8,9},{9,10},{10,1... | collective-permute-start | bytes 786440 | tf_op jit(solution)/shard_map/while/body/eval_jaxpr/ppermute | solution.py:22
  254.6 12.1 %collective-permute-start = (bf16[128,1024]{1,0:T(8,128)(2,1)S(1)}, bf16[128,1024]{1,0:T(8,128)(2,1)S(1)}, u32[]{:S(2)}, u32[]{:S(2)}) collective-permute-start(bf16[128,1024]{1,0:T(8,128)(2,1)S(1)} %get-tuple-element.321), channel_id=1, source_target_pairs={{0,1},{1,2},{2,3},{3,4},{4,5},{5,6},{6,7},{7,8},{8,9},{9,10},{10,1... | collective-permute-start | bytes 786440 | tf_op jit(solution)/shard_map/while/body/eval_jaxpr/ppermute | solution.py:22
  256.5 15.8 %collective-permute-start.1 = (bf16[128,1024]{1,0:T(8,128)(2,1)}, bf16[128,1024]{1,0:T(8,128)(2,1)S(1)}, u32[]{:S(2)}, u32[]{:S(2)}) collective-permute-start(bf16[128,1024]{1,0:T(8,128)(2,1)} %get-tuple-element.322), channel_id=1, source_target_pairs={{0,1},{1,2},{2,3},{3,4},{4,5},{5,6},{6,7},{7,8},{8,9},{9,10},{10,1... | collective-permute-start | bytes 786440 | tf_op jit(solution)/shard_map/while/body/eval_jaxpr/ppermute | solution.py:22
  275.0 11.2 %collective-permute-start = (bf16[128,1024]{1,0:T(8,128)(2,1)S(1)}, bf16[128,1024]{1,0:T(8,128)(2,1)S(1)}, u32[]{:S(2)}, u32[]{:S(2)}) collective-permute-start(bf16[128,1024]{1,0:T(8,128)(2,1)S(1)} %get-tuple-element.321), channel_id=1, source_target_pairs={{0,1},{1,2},{2,3},{3,4},{4,5},{5,6},{6,7},{7,8},{8,9},{9,10},{10,1... | collective-permute-start | bytes 786440 | tf_op jit(solution)/shard_map/while/body/eval_jaxpr/ppermute | solution.py:22
  276.9 14.9 %collective-permute-start.1 = (bf16[128,1024]{1,0:T(8,128)(2,1)}, bf16[128,1024]{1,0:T(8,128)(2,1)S(1)}, u32[]{:S(2)}, u32[]{:S(2)}) collective-permute-start(bf16[128,1024]{1,0:T(8,128)(2,1)} %get-tuple-element.322), channel_id=1, source_target_pairs={{0,1},{1,2},{2,3},{3,4},{4,5},{5,6},{6,7},{7,8},{8,9},{9,10},{10,1... | collective-permute-start | bytes 786440 | tf_op jit(solution)/shard_map/while/body/eval_jaxpr/ppermute | solution.py:22
  294.6 10.3 %collective-permute-start = (bf16[128,1024]{1,0:T(8,128)(2,1)S(1)}, bf16[128,1024]{1,0:T(8,128)(2,1)S(1)}, u32[]{:S(2)}, u32[]{:S(2)}) collective-permute-start(bf16[128,1024]{1,0:T(8,128)(2,1)S(1)} %get-tuple-element.321), channel_id=1, source_target_pairs={{0,1},{1,2},{2,3},{3,4},{4,5},{5,6},{6,7},{7,8},{8,9},{9,10},{10,1... | collective-permute-start | bytes 786440 | tf_op jit(solution)/shard_map/while/body/eval_jaxpr/ppermute | solution.py:22
  296.5 14.0 %collective-permute-start.1 = (bf16[128,1024]{1,0:T(8,128)(2,1)}, bf16[128,1024]{1,0:T(8,128)(2,1)S(1)}, u32[]{:S(2)}, u32[]{:S(2)}) collective-permute-start(bf16[128,1024]{1,0:T(8,128)(2,1)} %get-tuple-element.322), channel_id=1, source_target_pairs={{0,1},{1,2},{2,3},{3,4},{4,5},{5,6},{6,7},{7,8},{8,9},{9,10},{10,1... | collective-permute-start | bytes 786440 | tf_op jit(solution)/shard_map/while/body/eval_jaxpr/ppermute | solution.py:22
  313.2 9.2 %collective-permute-start = (bf16[128,1024]{1,0:T(8,128)(2,1)S(1)}, bf16[128,1024]{1,0:T(8,128)(2,1)S(1)}, u32[]{:S(2)}, u32[]{:S(2)}) collective-permute-start(bf16[128,1024]{1,0:T(8,128)(2,1)S(1)} %get-tuple-element.321), channel_id=1, source_target_pairs={{0,1},{1,2},{2,3},{3,4},{4,5},{5,6},{6,7},{7,8},{8,9},{9,10},{10,1... | collective-permute-start | bytes 786440 | tf_op jit(solution)/shard_map/while/body/eval_jaxpr/ppermute | solution.py:22
  315.1 13.1 %collective-permute-start.1 = (bf16[128,1024]{1,0:T(8,128)(2,1)}, bf16[128,1024]{1,0:T(8,128)(2,1)S(1)}, u32[]{:S(2)}, u32[]{:S(2)}) collective-permute-start(bf16[128,1024]{1,0:T(8,128)(2,1)} %get-tuple-element.322), channel_id=1, source_target_pairs={{0,1},{1,2},{2,3},{3,4},{4,5},{5,6},{6,7},{7,8},{8,9},{9,10},{10,1... | collective-permute-start | bytes 786440 | tf_op jit(solution)/shard_map/while/body/eval_jaxpr/ppermute | solution.py:22
  330.9 9.2 %collective-permute-start = (bf16[128,1024]{1,0:T(8,128)(2,1)S(1)}, bf16[128,1024]{1,0:T(8,128)(2,1)S(1)}, u32[]{:S(2)}, u32[]{:S(2)}) collective-permute-start(bf16[128,1024]{1,0:T(8,128)(2,1)S(1)} %get-tuple-element.321), channel_id=1, source_target_pairs={{0,1},{1,2},{2,3},{3,4},{4,5},{5,6},{6,7},{7,8},{8,9},{9,10},{10,1... | collective-permute-start | bytes 786440 | tf_op jit(solution)/shard_map/while/body/eval_jaxpr/ppermute | solution.py:22
  332.9 12.1 %collective-permute-start.1 = (bf16[128,1024]{1,0:T(8,128)(2,1)}, bf16[128,1024]{1,0:T(8,128)(2,1)S(1)}, u32[]{:S(2)}, u32[]{:S(2)}) collective-permute-start(bf16[128,1024]{1,0:T(8,128)(2,1)} %get-tuple-element.322), channel_id=1, source_target_pairs={{0,1},{1,2},{2,3},{3,4},{4,5},{5,6},{6,7},{7,8},{8,9},{9,10},{10,1... | collective-permute-start | bytes 786440 | tf_op jit(solution)/shard_map/while/body/eval_jaxpr/ppermute | solution.py:22
  347.7 9.2 %collective-permute-start = (bf16[128,1024]{1,0:T(8,128)(2,1)S(1)}, bf16[128,1024]{1,0:T(8,128)(2,1)S(1)}, u32[]{:S(2)}, u32[]{:S(2)}) collective-permute-start(bf16[128,1024]{1,0:T(8,128)(2,1)S(1)} %get-tuple-element.321), channel_id=1, source_target_pairs={{0,1},{1,2},{2,3},{3,4},{4,5},{5,6},{6,7},{7,8},{8,9},{9,10},{10,1... | collective-permute-start | bytes 786440 | tf_op jit(solution)/shard_map/while/body/eval_jaxpr/ppermute | solution.py:22
  349.7 11.2 %collective-permute-start.1 = (bf16[128,1024]{1,0:T(8,128)(2,1)}, bf16[128,1024]{1,0:T(8,128)(2,1)S(1)}, u32[]{:S(2)}, u32[]{:S(2)}) collective-permute-start(bf16[128,1024]{1,0:T(8,128)(2,1)} %get-tuple-element.322), channel_id=1, source_target_pairs={{0,1},{1,2},{2,3},{3,4},{4,5},{5,6},{6,7},{7,8},{8,9},{9,10},{10,1... | collective-permute-start | bytes 786440 | tf_op jit(solution)/shard_map/while/body/eval_jaxpr/ppermute | solution.py:22
  363.6 9.2 %collective-permute-start = (bf16[128,1024]{1,0:T(8,128)(2,1)S(1)}, bf16[128,1024]{1,0:T(8,128)(2,1)S(1)}, u32[]{:S(2)}, u32[]{:S(2)}) collective-permute-start(bf16[128,1024]{1,0:T(8,128)(2,1)S(1)} %get-tuple-element.321), channel_id=1, source_target_pairs={{0,1},{1,2},{2,3},{3,4},{4,5},{5,6},{6,7},{7,8},{8,9},{9,10},{10,1... | collective-permute-start | bytes 786440 | tf_op jit(solution)/shard_map/while/body/eval_jaxpr/ppermute | solution.py:22
  365.5 10.1 %collective-permute-start.1 = (bf16[128,1024]{1,0:T(8,128)(2,1)}, bf16[128,1024]{1,0:T(8,128)(2,1)S(1)}, u32[]{:S(2)}, u32[]{:S(2)}) collective-permute-start(bf16[128,1024]{1,0:T(8,128)(2,1)} %get-tuple-element.322), channel_id=1, source_target_pairs={{0,1},{1,2},{2,3},{3,4},{4,5},{5,6},{6,7},{7,8},{8,9},{9,10},{10,1... | collective-permute-start | bytes 786440 | tf_op jit(solution)/shard_map/while/body/eval_jaxpr/ppermute | solution.py:22
  378.4 9.4 %collective-permute-start = (bf16[128,1024]{1,0:T(8,128)(2,1)S(1)}, bf16[128,1024]{1,0:T(8,128)(2,1)S(1)}, u32[]{:S(2)}, u32[]{:S(2)}) collective-permute-start(bf16[128,1024]{1,0:T(8,128)(2,1)S(1)} %get-tuple-element.321), channel_id=1, source_target_pairs={{0,1},{1,2},{2,3},{3,4},{4,5},{5,6},{6,7},{7,8},{8,9},{9,10},{10,1... | collective-permute-start | bytes 786440 | tf_op jit(solution)/shard_map/while/body/eval_jaxpr/ppermute | solution.py:22
  380.3 10.3 %collective-permute-start.1 = (bf16[128,1024]{1,0:T(8,128)(2,1)}, bf16[128,1024]{1,0:T(8,128)(2,1)S(1)}, u32[]{:S(2)}, u32[]{:S(2)}) collective-permute-start(bf16[128,1024]{1,0:T(8,128)(2,1)} %get-tuple-element.322), channel_id=1, source_target_pairs={{0,1},{1,2},{2,3},{3,4},{4,5},{5,6},{6,7},{7,8},{8,9},{9,10},{10,1... | collective-permute-start | bytes 786440 | tf_op jit(solution)/shard_map/while/body/eval_jaxpr/ppermute | solution.py:22
  393.3 9.2 %collective-permute-start = (bf16[128,1024]{1,0:T(8,128)(2,1)S(1)}, bf16[128,1024]{1,0:T(8,128)(2,1)S(1)}, u32[]{:S(2)}, u32[]{:S(2)}) collective-permute-start(bf16[128,1024]{1,0:T(8,128)(2,1)S(1)} %get-tuple-element.321), channel_id=1, source_target_pairs={{0,1},{1,2},{2,3},{3,4},{4,5},{5,6},{6,7},{7,8},{8,9},{9,10},{10,1... | collective-permute-start | bytes 786440 | tf_op jit(solution)/shard_map/while/body/eval_jaxpr/ppermute | solution.py:22
  395.2 10.1 %collective-permute-start.1 = (bf16[128,1024]{1,0:T(8,128)(2,1)}, bf16[128,1024]{1,0:T(8,128)(2,1)S(1)}, u32[]{:S(2)}, u32[]{:S(2)}) collective-permute-start(bf16[128,1024]{1,0:T(8,128)(2,1)} %get-tuple-element.322), channel_id=1, source_target_pairs={{0,1},{1,2},{2,3},{3,4},{4,5},{5,6},{6,7},{7,8},{8,9},{9,10},{10,1... | collective-permute-start | bytes 786440 | tf_op jit(solution)/shard_map/while/body/eval_jaxpr/ppermute | solution.py:22
  408.1 9.2 %collective-permute-start = (bf16[128,1024]{1,0:T(8,128)(2,1)S(1)}, bf16[128,1024]{1,0:T(8,128)(2,1)S(1)}, u32[]{:S(2)}, u32[]{:S(2)}) collective-permute-start(bf16[128,1024]{1,0:T(8,128)(2,1)S(1)} %get-tuple-element.321), channel_id=1, source_target_pairs={{0,1},{1,2},{2,3},{3,4},{4,5},{5,6},{6,7},{7,8},{8,9},{9,10},{10,1... | collective-permute-start | bytes 786440 | tf_op jit(solution)/shard_map/while/body/eval_jaxpr/ppermute | solution.py:22
  410.0 10.1 %collective-permute-start.1 = (bf16[128,1024]{1,0:T(8,128)(2,1)}, bf16[128,1024]{1,0:T(8,128)(2,1)S(1)}, u32[]{:S(2)}, u32[]{:S(2)}) collective-permute-start(bf16[128,1024]{1,0:T(8,128)(2,1)} %get-tuple-element.322), channel_id=1, source_target_pairs={{0,1},{1,2},{2,3},{3,4},{4,5},{5,6},{6,7},{7,8},{8,9},{9,10},{10,1... | collective-permute-start | bytes 786440 | tf_op jit(solution)/shard_map/while/body/eval_jaxpr/ppermute | solution.py:22
  422.9 9.2 %collective-permute-start = (bf16[128,1024]{1,0:T(8,128)(2,1)S(1)}, bf16[128,1024]{1,0:T(8,128)(2,1)S(1)}, u32[]{:S(2)}, u32[]{:S(2)}) collective-permute-start(bf16[128,1024]{1,0:T(8,128)(2,1)S(1)} %get-tuple-element.321), channel_id=1, source_target_pairs={{0,1},{1,2},{2,3},{3,4},{4,5},{5,6},{6,7},{7,8},{8,9},{9,10},{10,1... | collective-permute-start | bytes 786440 | tf_op jit(solution)/shard_map/while/body/eval_jaxpr/ppermute | solution.py:22
  424.8 10.1 %collective-permute-start.1 = (bf16[128,1024]{1,0:T(8,128)(2,1)}, bf16[128,1024]{1,0:T(8,128)(2,1)S(1)}, u32[]{:S(2)}, u32[]{:S(2)}) collective-permute-start(bf16[128,1024]{1,0:T(8,128)(2,1)} %get-tuple-element.322), channel_id=1, source_target_pairs={{0,1},{1,2},{2,3},{3,4},{4,5},{5,6},{6,7},{7,8},{8,9},{9,10},{10,1... | collective-permute-start | bytes 786440 | tf_op jit(solution)/shard_map/while/body/eval_jaxpr/ppermute | solution.py:22
  437.6 10.2 %collective-permute-start = (bf16[128,1024]{1,0:T(8,128)(2,1)S(1)}, bf16[128,1024]{1,0:T(8,128)(2,1)S(1)}, u32[]{:S(2)}, u32[]{:S(2)}) collective-permute-start(bf16[128,1024]{1,0:T(8,128)(2,1)S(1)} %get-tuple-element.321), channel_id=1, source_target_pairs={{0,1},{1,2},{2,3},{3,4},{4,5},{5,6},{6,7},{7,8},{8,9},{9,10},{10,1... | collective-permute-start | bytes 786440 | tf_op jit(solution)/shard_map/while/body/eval_jaxpr/ppermute | solution.py:22
  439.5 11.1 %collective-permute-start.1 = (bf16[128,1024]{1,0:T(8,128)(2,1)}, bf16[128,1024]{1,0:T(8,128)(2,1)S(1)}, u32[]{:S(2)}, u32[]{:S(2)}) collective-permute-start(bf16[128,1024]{1,0:T(8,128)(2,1)} %get-tuple-element.322), channel_id=1, source_target_pairs={{0,1},{1,2},{2,3},{3,4},{4,5},{5,6},{6,7},{7,8},{8,9},{9,10},{10,1... | collective-permute-start | bytes 786440 | tf_op jit(solution)/shard_map/while/body/eval_jaxpr/ppermute | solution.py:22
  453.4 11.2 %collective-permute-start = (bf16[128,1024]{1,0:T(8,128)(2,1)S(1)}, bf16[128,1024]{1,0:T(8,128)(2,1)S(1)}, u32[]{:S(2)}, u32[]{:S(2)}) collective-permute-start(bf16[128,1024]{1,0:T(8,128)(2,1)S(1)} %get-tuple-element.321), channel_id=1, source_target_pairs={{0,1},{1,2},{2,3},{3,4},{4,5},{5,6},{6,7},{7,8},{8,9},{9,10},{10,1... | collective-permute-start | bytes 786440 | tf_op jit(solution)/shard_map/while/body/eval_jaxpr/ppermute | solution.py:22
  455.3 12.1 %collective-permute-start.1 = (bf16[128,1024]{1,0:T(8,128)(2,1)}, bf16[128,1024]{1,0:T(8,128)(2,1)S(1)}, u32[]{:S(2)}, u32[]{:S(2)}) collective-permute-start(bf16[128,1024]{1,0:T(8,128)(2,1)} %get-tuple-element.322), channel_id=1, source_target_pairs={{0,1},{1,2},{2,3},{3,4},{4,5},{5,6},{6,7},{7,8},{8,9},{9,10},{10,1... | collective-permute-start | bytes 786440 | tf_op jit(solution)/shard_map/while/body/eval_jaxpr/ppermute | solution.py:22
  470.2 12.4 %collective-permute-start = (bf16[128,1024]{1,0:T(8,128)(2,1)S(1)}, bf16[128,1024]{1,0:T(8,128)(2,1)S(1)}, u32[]{:S(2)}, u32[]{:S(2)}) collective-permute-start(bf16[128,1024]{1,0:T(8,128)(2,1)S(1)} %get-tuple-element.321), channel_id=1, source_target_pairs={{0,1},{1,2},{2,3},{3,4},{4,5},{5,6},{6,7},{7,8},{8,9},{9,10},{10,1... | collective-permute-start | bytes 786440 | tf_op jit(solution)/shard_map/while/body/eval_jaxpr/ppermute | solution.py:22
  472.1 13.2 %collective-permute-start.1 = (bf16[128,1024]{1,0:T(8,128)(2,1)}, bf16[128,1024]{1,0:T(8,128)(2,1)S(1)}, u32[]{:S(2)}, u32[]{:S(2)}) collective-permute-start(bf16[128,1024]{1,0:T(8,128)(2,1)} %get-tuple-element.322), channel_id=1, source_target_pairs={{0,1},{1,2},{2,3},{3,4},{4,5},{5,6},{6,7},{7,8},{8,9},{9,10},{10,1... | collective-permute-start | bytes 786440 | tf_op jit(solution)/shard_map/while/body/eval_jaxpr/ppermute | solution.py:22
  488.0 12.4 %collective-permute-start = (bf16[128,1024]{1,0:T(8,128)(2,1)S(1)}, bf16[128,1024]{1,0:T(8,128)(2,1)S(1)}, u32[]{:S(2)}, u32[]{:S(2)}) collective-permute-start(bf16[128,1024]{1,0:T(8,128)(2,1)S(1)} %get-tuple-element.321), channel_id=1, source_target_pairs={{0,1},{1,2},{2,3},{3,4},{4,5},{5,6},{6,7},{7,8},{8,9},{9,10},{10,1... | collective-permute-start | bytes 786440 | tf_op jit(solution)/shard_map/while/body/eval_jaxpr/ppermute | solution.py:22
  489.9 14.3 %collective-permute-start.1 = (bf16[128,1024]{1,0:T(8,128)(2,1)}, bf16[128,1024]{1,0:T(8,128)(2,1)S(1)}, u32[]{:S(2)}, u32[]{:S(2)}) collective-permute-start(bf16[128,1024]{1,0:T(8,128)(2,1)} %get-tuple-element.322), channel_id=1, source_target_pairs={{0,1},{1,2},{2,3},{3,4},{4,5},{5,6},{6,7},{7,8},{8,9},{9,10},{10,1... | collective-permute-start | bytes 786440 | tf_op jit(solution)/shard_map/while/body/eval_jaxpr/ppermute | solution.py:22
  507.0 12.2 %collective-permute-start = (bf16[128,1024]{1,0:T(8,128)(2,1)S(1)}, bf16[128,1024]{1,0:T(8,128)(2,1)S(1)}, u32[]{:S(2)}, u32[]{:S(2)}) collective-permute-start(bf16[128,1024]{1,0:T(8,128)(2,1)S(1)} %get-tuple-element.321), channel_id=1, source_target_pairs={{0,1},{1,2},{2,3},{3,4},{4,5},{5,6},{6,7},{7,8},{8,9},{9,10},{10,1... | collective-permute-start | bytes 786440 | tf_op jit(solution)/shard_map/while/body/eval_jaxpr/ppermute | solution.py:22
  508.9 15.4 %collective-permute-start.1 = (bf16[128,1024]{1,0:T(8,128)(2,1)}, bf16[128,1024]{1,0:T(8,128)(2,1)S(1)}, u32[]{:S(2)}, u32[]{:S(2)}) collective-permute-start(bf16[128,1024]{1,0:T(8,128)(2,1)} %get-tuple-element.322), channel_id=1, source_target_pairs={{0,1},{1,2},{2,3},{3,4},{4,5},{5,6},{6,7},{7,8},{8,9},{9,10},{10,1... | collective-permute-start | bytes 786440 | tf_op jit(solution)/shard_map/while/body/eval_jaxpr/ppermute | solution.py:22
  527.1 11.9 %collective-permute-start.3 = (bf16[128,1024]{1,0:T(8,128)(2,1)}, bf16[128,1024]{1,0:T(8,128)(2,1)S(1)}, u32[]{:S(2)}, u32[]{:S(2)}) collective-permute-start(bf16[128,1024]{1,0:T(8,128)(2,1)} %get-tuple-element.228), channel_id=1, source_target_pairs={{0,1},{1,2},{2,3},{3,4},{4,5},{5,6},{6,7},{7,8},{8,9},{9,10},{10,1... | collective-permute-start | bytes 786440 | tf_op jit(solution)/shard_map/ppermute | solution.py:22
  (1 other events, 5.8 us)
Sparse Core Ops, SparseCore 0:
  539.9 94.8 all-gather.2
